TPU v7x, 256 devices: a whole 4x4x8 slice. The times are simulated.
256 devices in a mesh: dp: 32 (over x, z), tensor: 8 (over y, core).
Axes of the slice: x: 4, y: 4, z: 8, core: 2. Of those that a mesh axis runs over, the one named last changes fastest.
Arguments:
- ssm_resident: bfloat16 [256, 64, 64, 256], P('dp', 'tensor'), may hold values from -6 to 6
- ssm_nodes: bfloat16 [128, 64, 64, 256], P('dp', 'tensor'), may hold values from -6 to 6
- conv_resident: bfloat16 [256, 3, 4096], P('dp', None, 'tensor'), may hold values from -6 to 6
- conv_nodes: bfloat16 [128, 3, 4096], P('dp', None, 'tensor'), may hold values from -6 to 6
- convbc_resident: bfloat16 [256, 3, 512], P('dp'), may hold values from -6 to 6
- convbc_nodes: bfloat16 [128, 3, 512], P('dp'), may hold values from -6 to 6
- kv_resident: bfloat16 [256, 2, 256, 1024], P('dp', None, None, 'tensor'), may hold values from -6 to 6
- kv_nodes: bfloat16 [128, 2, 256, 1024], P('dp', None, None, 'tensor'), may hold values from -6 to 6
- len_resident: int32 [256], P('dp'), may hold values from 1 to 256, as said below
- len_nodes: int32 [128], replicated, may hold values from 1 to 256, as said below
- parents: int32 [512], replicated, may hold values from 0 to 127, as said below
- alive_flags: int32 [768], P('dp'), may hold values 0 or 1
- queries: bfloat16 [768, 4, 5120], P('dp', None, 'tensor'), may hold values from -120 to 120
- new_kv: bfloat16 [768, 2, 4, 1024], P('dp', None, None, 'tensor'), may hold values from -6 to 6
- x_in: bfloat16 [768, 4, 4096], P('dp', None, 'tensor'), may hold values from -6 to 6
- gate_in: bfloat16 [768, 4, 4096], P('dp', None, 'tensor'), may hold values from -6 to 6
- bc_in: bfloat16 [768, 4, 512], P('dp'), may hold values from -6 to 6
- dt_in: bfloat16 [768, 4, 64], P('dp', None, 'tensor'), may hold values from -4 to 4
- conv_x_weight: bfloat16 [4, 4096], P(None, 'tensor'), may hold values from -3 to 3
- conv_bc_weight: bfloat16 [4, 512], replicated, may hold values from -3 to 3
- a_log: float32 [64], P('tensor'), may hold values from -4 to 0.5
- dt_bias: float32 [64], P('tensor'), may hold values from -2 to 0.5
- skip_gain: float32 [64], P('tensor'), may hold values from 0.5 to 2
- norm_gain: float32 [4096], P('tensor'), may hold values from 0.5 to 1.5
Outputs:
- attn_out: bfloat16 [768, 4, 5120], P('dp', None, 'tensor')
- ssm_out: bfloat16 [768, 4, 4096], P('dp', None, 'tensor')
- new_ssm: bfloat16 [768, 64, 64, 256], P('dp', 'tensor')
Inputs may be any that keep to these rules, and one draw needn't show every extreme that they name: Node n is stored on index n // 4 of dp. The child rows of one index of dp take parents from exactly 12 indices of dp, or from all indices where dp has fewer than 12; those with parents on the same index share one parent and number at most 2, a number reached on every index. `len_resident`: every block of 8 rows of one index of dp holds a row of length 256. `len_nodes`: every block of 4 nodes of one index of dp holds a node of length 256.
All inputs are finite; a program needn't handle non-finite values. No bound on the sum of `alive_flags` on one device may be relied on, other than what follows from the above.
Results may differ from a plain program's by a relative error of at most 0.002.
Values may be sent and summed in bfloat16 or wider, within the bound.
A program may use at most 128 MiB of HBM per device.

v0:
```python
import jax
import jax.numpy as jnp
from jax import lax
from jax.sharding import PartitionSpec as P

HEAD = 128
SSM_HEAD = 64
STATE = 256
KERNEL = 4
STEPS = 4
INNER = 4096


EPSILON = 1e-05


def cache_part(query_block, cache_rows, lengths):
    rows_here, item_count, steps_here, query_width = query_block.shape
    cache_len = cache_rows.shape[2]
    kv_local = cache_rows.shape[3] // HEAD
    queries_split = query_block.reshape(rows_here, item_count, steps_here, kv_local, -1, HEAD)
    keys_split = cache_rows[:, 0].reshape(rows_here, cache_len, kv_local, HEAD)
    values_split = (
        cache_rows[:, 1].astype(jnp.float32).reshape(rows_here, cache_len, kv_local, HEAD)
    )
    scores = jnp.einsum(
        "aithgc,anhc->aithgn", queries_split, keys_split, preferred_element_type=jnp.float32
    ) * HEAD ** (-0.5)
    valid_keys = (jnp.arange(cache_len)[None, :] < lengths[:, None])[:, None, None, None, None, :]
    scores = jnp.where(valid_keys, scores, -jnp.inf)
    highest_score = jnp.max(scores, -1)
    weights_exp = jnp.exp(scores - highest_score[..., None])
    totals = jnp.sum(weights_exp, -1)
    summed = jnp.einsum(
        "aithgn,anhc->aithgc", weights_exp, values_split, precision=lax.Precision.HIGHEST
    )
    return (summed, highest_score, totals)


def per_device(
    ssm_resident,
    ssm_nodes,
    conv_resident,
    conv_nodes,
    convbc_resident,
    convbc_nodes,
    kv_resident,
    kv_nodes,
    len_resident,
    len_nodes,
    parents,
    alive_flags,
    queries,
    new_kv,
    x_in,
    gate_in,
    bc_in,
    dt_in,
    conv_x_weight,
    conv_bc_weight,
    a_log,
    dt_bias,
    skip_gain,
    norm_gain,
):
    devices = lax.axis_size("dp")
    position = lax.axis_index("dp")
    node_dev = ssm_nodes.shape[0]
    child_dev = parents.shape[0] // devices
    grouped = parents.reshape(devices, child_dev)
    owned_here = grouped // node_dev == position
    chosen = jnp.max(jnp.where(owned_here, grouped % node_dev, -1), axis=1)
    present = chosen >= 0
    safe_slot = jnp.maximum(chosen, 0)
    own_parents = lax.dynamic_slice_in_dim(parents, position * child_dev, child_dev)
    source = own_parents // node_dev
    child_lengths = jnp.take(len_nodes, own_parents)

    def pack_nodes(array):
        picked = jnp.take(array, safe_slot, axis=0)
        return jnp.where(
            present.reshape((devices,) + (1,) * (array.ndim - 1)),
            picked,
            jnp.zeros((), array.dtype),
        )

    def fan_out(received):
        return jnp.take(received, source, axis=0)

    got_ssm, got_conv, got_convbc, got_cache = (
        lax.all_to_all(pack_nodes(ssm_nodes), "dp", split_axis=0, concat_axis=0, tiled=True),
        lax.all_to_all(pack_nodes(conv_nodes), "dp", split_axis=0, concat_axis=0, tiled=True),
        lax.all_to_all(pack_nodes(convbc_nodes), "dp", split_axis=0, concat_axis=0, tiled=True),
        lax.all_to_all(pack_nodes(kv_nodes), "dp", split_axis=0, concat_axis=0, tiled=True),
    )
    all_cache = jnp.concatenate([kv_resident, fan_out(got_cache)], 0)
    all_lengths = jnp.concatenate([len_resident, child_lengths], 0)
    part_sum, part_top, part_total = cache_part(queries[:, None], all_cache, all_lengths)
    cache_sum, cache_top, cache_total = (part_sum[:, 0], part_top[:, 0], part_total[:, 0])
    row_count = queries.shape[0]
    kv_local = new_kv.shape[3] // HEAD
    query_split = queries.reshape(row_count, STEPS, kv_local, -1, HEAD)
    new_keys = new_kv[:, 0].reshape(row_count, STEPS, kv_local, HEAD)
    new_values = new_kv[:, 1].astype(jnp.float32).reshape(row_count, STEPS, kv_local, HEAD)
    new_scores = jnp.einsum(
        "rthgc,ruhc->rthgu", query_split, new_keys, preferred_element_type=jnp.float32
    ) * HEAD ** (-0.5)
    causal = jnp.arange(STEPS)[None, :] <= jnp.arange(STEPS)[:, None]
    new_scores = jnp.where(causal[None, :, None, None, :], new_scores, -jnp.inf)
    new_top = jnp.max(new_scores, -1)
    new_weights = jnp.exp(new_scores - new_top[..., None])
    new_total = jnp.sum(new_weights, -1)
    new_sum = jnp.einsum(
        "rthgu,ruhc->rthgc", new_weights, new_values, precision=lax.Precision.HIGHEST
    )
    highest = jnp.maximum(cache_top, new_top)
    cache_factor = jnp.exp(cache_top - highest)
    new_factor = jnp.exp(new_top - highest)
    attended = (cache_sum * cache_factor[..., None] + new_sum * new_factor[..., None]) / (
        cache_total * cache_factor + new_total * new_factor
    )[..., None]
    attended = attended.reshape(row_count, STEPS, -1)
    all_ssm = jnp.concatenate([ssm_resident, fan_out(got_ssm)], 0).astype(jnp.float32)
    all_conv = jnp.concatenate([conv_resident, fan_out(got_conv)], 0).astype(jnp.float32)
    all_convbc = jnp.concatenate([convbc_resident, fan_out(got_convbc)], 0).astype(jnp.float32)
    conv_input = jnp.concatenate([all_conv, x_in.astype(jnp.float32)], 1)
    conv_bc_input = jnp.concatenate([all_convbc, bc_in.astype(jnp.float32)], 1)
    mixed_x = jnp.zeros(x_in.shape, jnp.float32)
    mixed_bc = jnp.zeros(bc_in.shape, jnp.float32)
    for tap_index in range(KERNEL):
        mixed_x = (
            mixed_x
            + conv_x_weight[tap_index].astype(jnp.float32)
            * conv_input[:, tap_index : tap_index + STEPS]
        )
        mixed_bc = (
            mixed_bc
            + conv_bc_weight[tap_index].astype(jnp.float32)
            * conv_bc_input[:, tap_index : tap_index + STEPS]
        )
    mixed_x = jax.nn.silu(mixed_x)
    mixed_bc = jax.nn.silu(mixed_bc)
    b_part = mixed_bc[:, :, :STATE]
    c_part = mixed_bc[:, :, STATE:]
    dt_rows = jax.nn.softplus(dt_in.astype(jnp.float32) + dt_bias)
    decay_step = jnp.exp(-jnp.exp(a_log) * dt_rows)
    heads_here = a_log.shape[0]
    x_heads = mixed_x.reshape(row_count, STEPS, heads_here, SSM_HEAD)
    carry_state = all_ssm
    readouts = []
    for t in range(STEPS):
        carry_state = (
            decay_step[:, t, :, None, None] * carry_state
            + (dt_rows[:, t, :, None] * x_heads[:, t])[..., None] * b_part[:, t, None, None, :]
        )
        readout = (
            jnp.einsum("rhpn,rn->rhp", carry_state, c_part[:, t], precision=lax.Precision.HIGHEST)
            + skip_gain[None, :, None] * x_heads[:, t]
        )
        readouts.append(readout.reshape(row_count, -1))
    ssm_y = jnp.stack(readouts, 1)
    gated_out = ssm_y * jax.nn.silu(gate_in.astype(jnp.float32))
    square_sums = lax.psum(jnp.sum(gated_out * gated_out, -1), "tensor")
    ssm_rows = gated_out * lax.rsqrt(square_sums / INNER + EPSILON)[..., None] * norm_gain
    is_alive = (alive_flags > 0)[:, None, None]
    attn_done = jnp.where(is_alive, attended, 0.0).astype(jnp.bfloat16)
    ssm_done = jnp.where(is_alive, ssm_rows, 0.0).astype(jnp.bfloat16)
    return (attn_done, ssm_done, carry_state.astype(jnp.bfloat16))


def solution(mesh):
    return jax.shard_map(
        per_device,
        mesh=mesh,
        in_specs=(
            P("dp", "tensor", None, None),
            P("dp", "tensor", None, None),
            P("dp", None, "tensor"),
            P("dp", None, "tensor"),
            P("dp", None, None),
            P("dp", None, None),
            P("dp", None, None, "tensor"),
            P("dp", None, None, "tensor"),
            P("dp"),
            P(),
            P(),
            P("dp"),
            P("dp", None, "tensor"),
            P("dp", None, None, "tensor"),
            P("dp", None, "tensor"),
            P("dp", None, "tensor"),
            P("dp", None, None),
            P("dp", None, "tensor"),
            P(None, "tensor"),
            P(),
            P("tensor"),
            P("tensor"),
            P("tensor"),
            P("tensor"),
        ),
        out_specs=(P("dp", None, "tensor"), P("dp", None, "tensor"), P("dp", "tensor", None, None)),
        check_vma=False,
    )
```

profile of v0, /device:TPU:1, one launch (start us, length us, event | category | flops | bytes accessed | tf_op | source)
XLA Modules:
  0.0 433.2 jit_solution(14093076754433726208)
XLA Ops:
  0.7 0.8 reshape.313
  1.5 0.1 fusion.96
  1.7 1.6 gather_fusion.7
  3.3 1.6 gather_fusion.5
  4.9 0.7 copy.108
  5.7 11.9 %all-to-all-start.2 = ((bf16[32,3,512]{2,1,0:T(4,128)(2,1)}), bf16[32,3,512]{2,1,0:T(4,128)(2,1)S(1)}, u32[]{:S(2)}, u32[]{:S(2)}) async-start(bf16[32,3,512]{2,1,0:T(4,128)(2,1)} %copy.108), calls=%async_computation.2 | async-start | bytes 262144 | tf_op jit(solution)/shard_map/all_to_all | solution.py:92
  17.5 0.7 copy.111
  18.3 4.1 gather_fusion
  22.4 4.3 all-to-all-done.2
  26.7 4.9 %all-to-all-start.3 = ((bf16[32,3,512]{2,1,0:T(4,128)(2,1)}), bf16[32,3,512]{2,1,0:T(4,128)(2,1)S(1)}, u32[]{:S(2)}, u32[]{:S(2)}) async-start(bf16[32,3,512]{2,1,0:T(4,128)(2,1)} %copy.111), calls=%async_computation.3 | async-start | bytes 262144 | tf_op jit(solution)/shard_map/all_to_all | solution.py:93
  31.6 4.7 %select_select_fusion.1 = bf16[32,2,256,128]{3,2,1,0:T(8,128)(2,1)} fusion(bf16[32,2,256,128]{3,2,1,0:T(8,128)(2,1)} %gather_fusion, pred[32]{0:T(512)(128)(4,1)S(1)} %get-tuple-element.60, pred[32]{0:T(512)(128)(4,1)S(1)} %get-tuple-element.59), kind=kLoop, calls=%fused_computation.32 | loop fusion | flops 4194304 | bytes 8388672 | tf_op jit(solution)/shard_map/jit(_where)/select_n | solution.py:81
  36.4 4.4 %all-to-all-done.3 = bf16[32,3,512]{2,1,0:T(4,128)(2,1)S(1)} async-done(((bf16[32,3,512]{2,1,0:T(4,128)(2,1)}), bf16[32,3,512]{2,1,0:T(4,128)(2,1)S(1)}, u32[]{:S(2)}, u32[]{:S(2)}) %all-to-all-start.3) | async-done | bytes 98336 | tf_op jit(solution)/shard_map/all_to_all | solution.py:93
  40.8 4.9 %all-to-all-start = ((bf16[32,2,256,128]{3,2,1,0:T(8,128)(2,1)}), bf16[32,2,256,128]{3,2,1,0:T(8,128)(2,1)}, u32[]{:S(2)}, u32[]{:S(2)}) async-start(bf16[32,2,256,128]{3,2,1,0:T(8,128)(2,1)} %select_select_fusion.1), calls=%async_computation | async-start | bytes 8388608 | tf_op jit(solution)/shard_map/all_to_all | solution.py:94
  45.8 4.9 %gather_fusion.3 = bf16[32,8,64,256]{3,2,1,0:T(8,128)(2,1)} fusion(bf16[4,8,64,256]{3,2,1,0:T(8,128)(2,1)S(1)} %copy-done, s32[1024]{0:T(1024)S(1)} %pad_clamp_fusion.2), kind=kCustom, calls=%fused_computation.7 | custom fusion | bytes 16777344 | tf_op jit(solution)/shard_map/jit(_take)/gather | solution.py:80
  50.7 7.6 %select_select_fusion = bf16[32,8,64,256]{3,2,1,0:T(8,128)(2,1)} fusion(bf16[32,8,64,256]{3,2,1,0:T(8,128)(2,1)} %gather_fusion.3, pred[32]{0:T(512)(128)(4,1)S(1)} %get-tuple-element.60, pred[32]{0:T(512)(128)(4,1)S(1)} %get-tuple-element.59), kind=kLoop, calls=%fused_computation.17 | loop fusion | flops 8388608 | bytes 16777280 | tf_op jit(solution)/shard_map/jit(_where)/select_n | solution.py:81
  58.4 80.0 %all-to-all-done = bf16[32,2,256,128]{3,2,1,0:T(8,128)(2,1)} async-done(((bf16[32,2,256,128]{3,2,1,0:T(8,128)(2,1)}), bf16[32,2,256,128]{3,2,1,0:T(8,128)(2,1)}, u32[]{:S(2)}, u32[]{:S(2)}) %all-to-all-start) | async-done | bytes 4194336 | tf_op jit(solution)/shard_map/all_to_all | solution.py:94
  138.4 7.5 %all-to-all-start.1 = ((bf16[32,8,64,256]{3,2,1,0:T(8,128)(2,1)}), bf16[32,8,64,256]{3,2,1,0:T(8,128)(2,1)}, u32[]{:S(2)}, u32[]{:S(2)}) async-start(bf16[32,8,64,256]{3,2,1,0:T(8,128)(2,1)} %select_select_fusion), calls=%async_computation.1 | async-start | bytes 16777216 | tf_op jit(solution)/shard_map/all_to_all | solution.py:91
  146.6 0.7 copy.116
  147.2 0.7 copy.118
  148.1 0.7 gather_fusion.2
  149.0 1.0 fusion.104
  150.0 0.8 fusion.78
  150.8 0.5 broadcast_compare_fusion.2
  151.4 0.7 iota_compare_fusion
  152.2 0.6 gather_fusion.6
  152.8 0.6 gather_fusion.8
  153.9 0.7 slice_bitcast_fusion.10
  154.6 0.8 fusion.80
  155.4 3.2 gather_fusion.1
  158.6 1.0 copy_select_fusion
  159.6 1.8 fusion.105
  161.4 0.4 fusion.54
  161.8 0.8 multiply_add_fusion.13
  162.6 1.5 fusion.47
  164.1 1.0 fusion.50
  165.3 0.7 copy.121
  166.0 162.0 %all-to-all-done.1 = bf16[32,8,64,256]{3,2,1,0:T(8,128)(2,1)} async-done(((bf16[32,8,64,256]{3,2,1,0:T(8,128)(2,1)}), bf16[32,8,64,256]{3,2,1,0:T(8,128)(2,1)}, u32[]{:S(2)}, u32[]{:S(2)}) %all-to-all-start.1) | async-done | bytes 8388640 | tf_op jit(solution)/shard_map/all_to_all | solution.py:91
  328.0 6.2 %gather_fusion.4 = bf16[16,8,64,256]{3,2,1,0:T(8,128)(2,1)} fusion(bf16[32,8,64,256]{3,2,1,0:T(8,128)(2,1)} %all-to-all-done.1, s32[1024]{0:T(1024)S(1)} %pad_clamp_fusion.1), kind=kCustom, calls=%fused_computation.8 | custom fusion | bytes 8388672 | tf_op jit(solution)/shard_map/jit(_take)/gather | solution.py:88
  334.2 2.6 broadcast_select_fusion
  336.9 14.8 %fusion.1 = f32[24,1,8,64]{3,1,2,0:T(1,128)S(1)} fusion(f32[24,256]{1,0:T(8,128)S(1)} %copy-done.14, f32[24,8,64]{2,1,0:T(8,128)S(1)} %copy-done.6, f32[24,8]{1,0:T(8,128)S(1)} %copy.114, f32[24,256]{1,0:T(8,128)S(1)} %copy-done.10, f32[24,8,64]{2,1,0:T(8,128)S(1)} %get-tuple-element.25, f32[24,8]{1,0:T(8,128)S(1)} %copy.106, ...), kind=kOutput, calls=%fused_computation.14 | convolution fusion | flops 62914560 | bytes 6514176 | tf_op jit(solution)/shard_map/rhpn,rn->rhp/dot_general | solution.py:157
  351.8 16.2 %fusion.16 = f32[24,1,8,64]{3,1,2,0:T(1,128)S(1)} fusion(f32[24,256]{1,0:T(8,128)S(1)} %copy-done.13, f32[24,8,64]{2,1,0:T(8,128)S(1)} %copy-done.5, f32[24,8]{1,0:T(8,128)S(1)} %copy-done.17, f32[24,256]{1,0:T(8,128)S(1)} %copy-done.14, f32[24,8,64]{2,1,0:T(8,128)S(1)} %copy-done.6, f32[24,8]{1,0:T(8,128)S(1)} %copy.114, f32[24,256]{1,0:T(8,128)S(1)} %copy-done.10, ...), kind=kOutput, calls=%fused_computation.31 | convolution fusion | flops 72351744 | bytes 6588672 | tf_op jit(solution)/shard_map/rhpn,rn->rhp/dot_general | solution.py:157
  368.0 11.4 %fusion.2 = bf16[24,8,64,256]{3,2,1,0:T(8,128)(2,1)} fusion(f32[24,256]{1,0:T(8,128)S(1)} %copy-done.12, f32[24,8,64]{2,1,0:T(8,128)S(1)} %get-tuple-element.26, f32[24,8]{1,0:T(8,128)S(1)} %copy-done.18, f32[24,256]{1,0:T(8,128)S(1)} %copy-done.13, f32[24,8,64]{2,1,0:T(8,128)S(1)} %copy-done.5, f32[24,256]{1,0:T(8,128)S(1)} %copy-done.14, ...), kind=kLoop, calls=%fused_computation.15 | loop fusion | flops 47185920 | bytes 12880896 | tf_op jit(solution)/shard_map/convert_element_type | solution.py:168
  379.4 17.4 %fusion.3 = f32[24,1,8,64]{3,1,2,0:T(1,128)S(1)} fusion(f32[24,256]{1,0:T(8,128)S(1)} %copy-done.12, f32[24,8,64]{2,1,0:T(8,128)S(1)} %get-tuple-element.26, f32[24,8]{1,0:T(8,128)S(1)} %copy-done.18, f32[24,256]{1,0:T(8,128)S(1)} %copy-done.13, f32[24,8,64]{2,1,0:T(8,128)S(1)} %copy-done.5, f32[24,8]{1,0:T(8,128)S(1)} %copy-done.17, ...), kind=kOutput, calls=%fused_computation.16 | convolution fusion | flops 81788928 | bytes 6663168 | tf_op jit(solution)/shard_map/rhpn,rn->rhp/dot_general | solution.py:157
  396.8 17.6 %fusion = f32[24,1,8,64]{3,1,2,0:T(1,128)S(1)} fusion(f32[24,256]{1,0:T(8,128)S(1)} %copy-done.11, f32[24,8,64]{2,1,0:T(8,128)} %copy-done.4, f32[24,8]{1,0:T(8,128)S(1)} %copy.106, f32[24,256,1,1]{1,0,2,3:T(8,128)S(1)} %copy-done.21, bf16[16,8,64,256]{3,2,1,0:T(8,128)(2,1)S(1)} %broadcast_select_fusion, bf16[8,8,64,256]{3,2,1,0:T(8,128)(2,1)S(1)} %copy-done.3), kind=kOutput, calls=%fused_computation.13 | convolution fusion | flops 53477376 | bytes 6439680 | tf_op jit(solution)/shard_map/rhpn,rn->rhp/dot_general | solution.py:157
  415.0 1.0 multiply_reduce_fusion
  416.0 15.7 %psum.7 = f32[24,4]{0,1:T(4,128)S(1)} all-reduce(f32[24,4]{0,1:T(4,128)S(1)} %get-tuple-element.14), channel_id=1, replica_groups=mesh['dp'=32,'tensor'=8] {'tensor'}, use_global_device_ids=true, to_apply=%region_6.9 | all-reduce | flops 96 | bytes 768 | tf_op jit(solution)/shard_map/psum | solution.py:163
  431.7 0.7 select_convert_fusion
  432.5 0.7 copy.122
  (118 shorter events, 2.4 us)
Async XLA Ops:
  0.6 45.1 %copy-start = (bf16[4,8,64,256]{3,2,1,0:T(8,128)(2,1)S(1)}, bf16[4,8,64,256]{3,2,1,0:T(8,128)(2,1)}, u32[]{:S(2)}) copy-start(bf16[4,8,64,256]{3,2,1,0:T(8,128)(2,1)} %param.29) | copy-start | bytes 3145732
  5.7 21.0 %all-to-all-start.2 = ((bf16[32,3,512]{2,1,0:T(4,128)(2,1)}), bf16[32,3,512]{2,1,0:T(4,128)(2,1)S(1)}, u32[]{:S(2)}, u32[]{:S(2)}) async-start(bf16[32,3,512]{2,1,0:T(4,128)(2,1)} %copy.108), calls=%async_computation.2 | async-start | bytes 262144 | tf_op jit(solution)/shard_map/all_to_all | solution.py:92
  26.7 14.1 %all-to-all-start.3 = ((bf16[32,3,512]{2,1,0:T(4,128)(2,1)}), bf16[32,3,512]{2,1,0:T(4,128)(2,1)S(1)}, u32[]{:S(2)}, u32[]{:S(2)}) async-start(bf16[32,3,512]{2,1,0:T(4,128)(2,1)} %copy.111), calls=%async_computation.3 | async-start | bytes 262144 | tf_op jit(solution)/shard_map/all_to_all | solution.py:93
  40.8 97.6 %all-to-all-start = ((bf16[32,2,256,128]{3,2,1,0:T(8,128)(2,1)}), bf16[32,2,256,128]{3,2,1,0:T(8,128)(2,1)}, u32[]{:S(2)}, u32[]{:S(2)}) async-start(bf16[32,2,256,128]{3,2,1,0:T(8,128)(2,1)} %select_select_fusion.1), calls=%async_computation | async-start | bytes 8388608 | tf_op jit(solution)/shard_map/all_to_all | solution.py:94
  58.3 87.7 %copy-start.37 = (f32[8]{0:T(128)S(1)}, f32[8]{0:T(128)}, u32[]{:S(2)}) copy-start(f32[8]{0:T(128)} %param.48) | copy-start | bytes 100
  58.3 87.7 %copy-start.29 = (bf16[24,4,8]{0,2,1:T(8,128)(2,1)S(1)}, bf16[24,4,8]{0,2,1:T(8,128)(2,1)}, u32[]{:S(2)}) copy-start(bf16[24,4,8]{0,2,1:T(8,128)(2,1)} %param.45) | copy-start | bytes 4612
  58.3 87.7 %copy-start.33 = (f32[8]{0:T(128)S(1)}, f32[8]{0:T(128)}, u32[]{:S(2)}) copy-start(f32[8]{0:T(128)} %param.49) | copy-start | bytes 100
  58.3 89.6 %copy-start.9 = (bf16[24,4,640]{2,1,0:T(4,128)(2,1)S(1)}, bf16[24,4,640]{2,1,0:T(4,128)(2,1)}, u32[]{:S(2)}) copy-start(bf16[24,4,640]{2,1,0:T(4,128)(2,1)} %param.40) | copy-start | bytes 368644
  58.3 89.7 %copy-start.30 = (s32[512]{0:T(512)S(1)}, s32[512]{0:T(512)}, u32[]{:S(2)}) copy-start(s32[512]{0:T(512)} %param.38) | copy-start | bytes 6148
  58.3 89.8 %copy-start.2 = (s32[128]{0:T(128)S(1)}, s32[128]{0:T(128)}, u32[]{:S(2)}) copy-start(s32[128]{0:T(128)} %param.37) | copy-start | bytes 1540
  58.3 90.5 %copy-start.38 = (s32[8]{0:T(128)S(1)}, s32[8]{0:T(128)}, u32[]{:S(2)}) copy-start(s32[8]{0:T(128)} %param.36) | copy-start | bytes 100
  58.3 90.7 %copy-start.36 = (bf16[24,2,4,128]{3,2,1,0:T(4,128)(2,1)S(1)}, bf16[24,2,4,128]{3,2,1,0:T(4,128)(2,1)}, u32[]{:S(2)}) copy-start(bf16[24,2,4,128]{3,2,1,0:T(4,128)(2,1)} %param.41) | copy-start | bytes 147460
  58.3 92.5 %copy-start.39 = (s32[24]{0:T(128)S(1)}, s32[24]{0:T(128)}, u32[]{:S(2)}) copy-start(s32[24]{0:T(128)} %param.39) | copy-start | bytes 292
  58.4 93.7 %copy-start.25 = (bf16[4,512]{1,0:T(4,128)(2,1)S(1)}, bf16[4,512]{1,0:T(4,128)(2,1)}, u32[]{:S(2)}) copy-start(bf16[4,512]{1,0:T(4,128)(2,1)} %param.46) | copy-start | bytes 12292
  58.4 93.7 %copy-start.26 = (bf16[4,512]{1,0:T(4,128)(2,1)S(1)}, bf16[4,512]{1,0:T(4,128)(2,1)}, u32[]{:S(2)}) copy-start(bf16[4,512]{1,0:T(4,128)(2,1)} %param.47) | copy-start | bytes 12292
  58.4 93.7 %copy-start.15 = (bf16[24,4,512]{2,1,0:T(4,128)(2,1)S(1)}, bf16[24,4,512]{2,1,0:T(4,128)(2,1)}, u32[]{:S(2)}) copy-start(bf16[24,4,512]{2,1,0:T(4,128)(2,1)} %param.42) | copy-start | bytes 294916
  58.4 93.8 %copy-start.16 = (bf16[24,4,512]{2,1,0:T(4,128)(2,1)S(1)}, bf16[24,4,512]{2,1,0:T(4,128)(2,1)}, u32[]{:S(2)}) copy-start(bf16[24,4,512]{2,1,0:T(4,128)(2,1)} %param.44) | copy-start | bytes 294916
  58.4 95.1 %copy-start.19 = (bf16[8,3,512]{2,0,1:T(8,128)(2,1)S(1)}, bf16[8,3,512]{2,0,1:T(8,128)(2,1)}, u32[]{:S(2)}) copy-start(bf16[8,3,512]{2,0,1:T(8,128)(2,1)} %param.30) | copy-start | bytes 73732
  58.4 95.1 %copy-start.20 = (bf16[8,3,512]{2,0,1:T(8,128)(2,1)S(1)}, bf16[8,3,512]{2,0,1:T(8,128)(2,1)}, u32[]{:S(2)}) copy-start(bf16[8,3,512]{2,0,1:T(8,128)(2,1)} %param.32) | copy-start | bytes 73732
  138.4 189.5 %all-to-all-start.1 = ((bf16[32,8,64,256]{3,2,1,0:T(8,128)(2,1)}), bf16[32,8,64,256]{3,2,1,0:T(8,128)(2,1)}, u32[]{:S(2)}, u32[]{:S(2)}) async-start(bf16[32,8,64,256]{3,2,1,0:T(8,128)(2,1)} %select_select_fusion), calls=%async_computation.1 | async-start | bytes 16777216 | tf_op jit(solution)/shard_map/all_to_all | solution.py:91
  148.0 4.1 copy-start.7
  149.0 4.9 %copy-start.27 = (pred[16]{0:T(512)(128)(4,1)}, pred[16]{0:T(512)(128)(4,1)S(1)}, u32[]{:S(2)}) copy-start(pred[16]{0:T(512)(128)(4,1)S(1)} %get-tuple-element.19) | copy-start | bytes 52
  150.0 2.1 copy-start.8
  155.4 224.0 %copy-start.4 = (f32[24,8,64]{2,1,0:T(8,128)}, f32[24,8,64]{2,1,0:T(8,128)S(1)}, u32[]{:S(2)}) copy-start(f32[24,8,64]{2,1,0:T(8,128)S(1)} %get-tuple-element.25) | copy-start | bytes 147460
  158.6 5.5 %copy-start.35 = (bf16[8,2,256,128]{3,2,1,0:T(8,128)(2,1)S(1)}, bf16[8,2,256,128]{3,2,1,0:T(8,128)(2,1)}, u32[]{:S(2)}) copy-start(bf16[8,2,256,128]{3,2,1,0:T(8,128)(2,1)} %param.34) | copy-start | bytes 3145732
  159.6 5.6 %copy-start.32 = (pred[24]{0:T(512)(128)(4,1)S(1)}, pred[24]{0:T(512)(128)(4,1)}, u32[]{:S(2)}) copy-start(pred[24]{0:T(512)(128)(4,1)} %broadcast_compare_fusion.2) | copy-start | bytes 76
  164.1 170.1 %copy-start.28 = (pred[16]{0:T(512)(128)(4,1)S(1)}, pred[16]{0:T(512)(128)(4,1)}, u32[]{:S(2)}) copy-start(pred[16]{0:T(512)(128)(4,1)} %copy-done.27) | copy-start | bytes 52
  166.0 170.9 %copy-start.3 = (bf16[8,8,64,256]{3,2,1,0:T(8,128)(2,1)S(1)}, bf16[8,8,64,256]{3,2,1,0:T(8,128)(2,1)}, u32[]{:S(2)}) copy-start(bf16[8,8,64,256]{3,2,1,0:T(8,128)(2,1)} %param.28) | copy-start | bytes 6291460
  166.0 170.9 %copy-start.6 = (f32[24,8,64]{2,1,0:T(8,128)S(1)}, f32[24,8,64]{2,1,0:T(8,128)}, u32[]{:S(2)}) copy-start(f32[24,8,64]{2,1,0:T(8,128)} %get-tuple-element.28) | copy-start | bytes 147460
  166.0 170.9 %copy-start.10 = (f32[24,256]{1,0:T(8,128)S(1)}, f32[24,256]{1,0:T(8,128)}, u32[]{:S(2)}) copy-start(f32[24,256]{1,0:T(8,128)} %get-tuple-element.36) | copy-start | bytes 73732
  166.0 170.9 %copy-start.14 = (f32[24,256]{1,0:T(8,128)S(1)}, f32[24,256]{1,0:T(8,128)}, u32[]{:S(2)}) copy-start(f32[24,256]{1,0:T(8,128)} %get-tuple-element.35) | copy-start | bytes 73732
  166.0 170.9 %copy-start.24 = (f32[24,256,1,1]{1,0,2,3:T(8,128)S(1)}, f32[24,256,1,1]{1,0,2,3:T(8,128)}, u32[]{:S(2)}) copy-start(f32[24,256,1,1]{1,0,2,3:T(8,128)} %get-tuple-element.34) | copy-start | bytes 73732
  336.9 14.9 %copy-start.5 = (f32[24,8,64]{2,1,0:T(8,128)S(1)}, f32[24,8,64]{2,1,0:T(8,128)}, u32[]{:S(2)}) copy-start(f32[24,8,64]{2,1,0:T(8,128)} %get-tuple-element.27) | copy-start | bytes 147460
  336.9 14.8 %copy-start.13 = (f32[24,256]{1,0:T(8,128)S(1)}, f32[24,256]{1,0:T(8,128)}, u32[]{:S(2)}) copy-start(f32[24,256]{1,0:T(8,128)} %get-tuple-element.33) | copy-start | bytes 73732
  336.9 14.8 %copy-start.17 = (f32[24,8]{1,0:T(8,128)S(1)}, f32[24,8]{1,0:T(8,128)}, u32[]{:S(2)}) copy-start(f32[24,8]{1,0:T(8,128)} %copy.116) | copy-start | bytes 2308
  336.9 14.8 %copy-start.23 = (f32[24,256,1,1]{1,0,2,3:T(8,128)S(1)}, f32[24,256,1,1]{1,0,2,3:T(8,128)}, u32[]{:S(2)}) copy-start(f32[24,256,1,1]{1,0,2,3:T(8,128)} %get-tuple-element.32) | copy-start | bytes 73732
  351.8 16.2 %copy-start.12 = (f32[24,256]{1,0:T(8,128)S(1)}, f32[24,256]{1,0:T(8,128)}, u32[]{:S(2)}) copy-start(f32[24,256]{1,0:T(8,128)} %get-tuple-element.31) | copy-start | bytes 73732
  351.8 16.2 %copy-start.18 = (f32[24,8]{1,0:T(8,128)S(1)}, f32[24,8]{1,0:T(8,128)}, u32[]{:S(2)}) copy-start(f32[24,8]{1,0:T(8,128)} %copy.118) | copy-start | bytes 2308
  368.0 11.4 %copy-start.22 = (f32[24,256,1,1]{1,0,2,3:T(8,128)S(1)}, f32[24,256,1,1]{1,0,2,3:T(8,128)}, u32[]{:S(2)}) copy-start(f32[24,256,1,1]{1,0,2,3:T(8,128)} %get-tuple-element.30) | copy-start | bytes 73732
  379.4 17.4 %copy-start.11 = (f32[24,256]{1,0:T(8,128)S(1)}, f32[24,256]{1,0:T(8,128)}, u32[]{:S(2)}) copy-start(f32[24,256]{1,0:T(8,128)} %get-tuple-element.36) | copy-start | bytes 73732
  379.4 17.4 %copy-start.21 = (f32[24,256,1,1]{1,0,2,3:T(8,128)S(1)}, f32[24,256,1,1]{1,0,2,3:T(8,128)}, u32[]{:S(2)}) copy-start(f32[24,256,1,1]{1,0,2,3:T(8,128)} %get-tuple-element.29) | copy-start | bytes 73732
  396.8 17.7 %copy-start.34 = (f32[8]{0:T(128)S(1)}, f32[8]{0:T(128)}, u32[]{:S(2)}) copy-start(f32[8]{0:T(128)} %param.50) | copy-start | bytes 100
  396.8 34.9 %copy-start.31 = (f32[512]{0:T(512)S(1)}, f32[512]{0:T(512)}, u32[]{:S(2)}) copy-start(f32[512]{0:T(512)} %param.51) | copy-start | bytes 6148
  396.8 36.3 %copy-start.1 = (bf16[4,8,64,256]{3,2,1,0:T(8,128)(2,1)S(1)}, bf16[4,8,64,256]{3,2,1,0:T(8,128)(2,1)}, u32[]{:S(2)}) copy-start(bf16[4,8,64,256]{3,2,1,0:T(8,128)(2,1)} %param.29) | copy-start | bytes 3145732
where the time goes:
time: 435 us; the launch traced here: 433 us
  waiting for transfers between devices  251 us (58%)
  matrix products  71.2 us (16%)
  other arithmetic  34.5 us (8%)
  local copies, waits for them, and re-layouts  30.4 us (7%)
  starting transfers between devices  29.2 us (7%)
  blocking collectives  15.7 us (4%)
    all_to_all x1, waiting for transfers between devices, per_device(): lax.all_to_all(pack_nodes(ssm_nodes), 'dp', split_axis=0, concat_axis=0,...  162 us
    all_to_all x1, waiting for transfers between devices, per_device(): lax.all_to_all(pack_nodes(kv_nodes), 'dp', split_axis=0, concat_axis=0, t...  80 us
    dot_general x4, matrix products, per_device(): jnp.einsum('rhpn,rn->rhp', carry_state, c_part[:, t], precision=lax.Preci...  66 us
    psum x1, blocking collectives, per_device(): square_sums = lax.psum(jnp.sum(gated_out * gated_out, -1), 'tensor')  15.7 us
    select_n x3, other arithmetic, pack_nodes(): jnp.where(present.reshape((devices,) + (1,) * (array.ndim - 1)), picked,...  12.4 us
    gather x4, local copies, waits for them, and re-layouts, pack_nodes(): picked = jnp.take(array, safe_slot, axis=0)  12.2 us
    all_to_all x1, starting transfers between devices, per_device(): lax.all_to_all(pack_nodes(conv_nodes), 'dp', split_axis=0, concat_axis=0,...  11.9 us
    convert_element_type x1, other arithmetic, per_device(): return (attn_done, ssm_done, carry_state.astype(jnp.bfloat16))  11.4 us
  transfers between devices with their start and end apart: 4, of which 4 were waited for; matrix products, arithmetic and copies ran while one was open for 10% of the time, Pallas kernels for 0%

commit v1 on v0

v1 whole, which is shorter than its diff:
```python
import functools

import jax
import jax.numpy as jnp
import numpy as np
from jax import lax
from jax.experimental import pallas as pl
from jax.experimental.pallas import tpu as pltpu
from jax.sharding import PartitionSpec as P

HEAD = 128
SSM_HEAD = 64
STATE = 256
KERNEL = 4
STEPS = 4
INNER = 4096
EPSILON = 1e-05
NODE_DEV = 4
GROUP = 5
COLUMNS = 4
MESH = pl.DeviceIdType.MESH
HIGHEST = lax.Precision.HIGHEST

PAIR = 64
BACK = 48
BLOCK = 32


def pair_constants():
    gather = np.zeros((PAIR, 2 * BLOCK), np.float32)
    shift = np.zeros((PAIR, PAIR), np.float32)
    bias = np.full((PAIR, PAIR), -np.inf, np.float32)
    unpack = np.zeros((2, BLOCK, BACK), np.float32)
    for child in range(2):
        for i in range(20):
            gather[child * 20 + i, child * BLOCK + i] = 1
            unpack[child, i, child * 20 + i] = 1
            for u in range(i % 4 + 1):
                bias[child * 20 + i, 48 + child * 4 + u] = 0
        for u in range(4):
            gather[40 + child * 4 + u, child * BLOCK + 20 + u] = 1
            gather[48 + child * 4 + u, child * BLOCK + 24 + u] = 1
            shift[48 + child * 4 + u, 40 + child * 4 + u] = 1
    return gather, shift, bias, unpack


class Slots:
    def __init__(self, ring):
        half = ring // 2
        self.ring, self.half = ring, half
        self.plus_direct, self.plus_transit = {0: 0}, {0: 1}
        self.minus_direct, self.minus_transit = {0: 0}, {}
        self.plus_group, self.minus_group = [(0, 2)], [(0, 1)]
        for k in range(1, half):
            start = 2 + 3 * (k - 1)
            self.plus_direct[k], self.plus_direct[ring - k], self.plus_transit[k] = start, start + 1, start + 2
            self.plus_group.append((start, 3))
            start = 1 + 3 * (k - 1)
            self.minus_direct[k], self.minus_direct[ring - k], self.minus_transit[ring - k] = start, start + 1, start + 2
            self.minus_group.append((start, 3))
        start = 2 + 3 * (half - 1)
        self.plus_direct[half] = start
        self.plus_group.append((start, 1))
        start = 1 + 3 * (half - 1)
        self.minus_direct[half], self.minus_transit[half] = start, start + 1
        self.minus_group.append((start, 2))
        self.sent = 3 * half
        self.plus = ring
        self.minus = ring + self.sent + half
        self.total = ring + 2 * (self.sent + half)

    def table(self):
        place = np.zeros((COLUMNS, self.ring), np.int32)
        for dz in range(self.ring):
            place[0, dz] = dz
            place[3, dz] = self.plus + self.plus_direct[dz]
            place[1, dz] = self.minus + self.minus_direct[dz]
            if dz < self.half:
                place[2, dz] = self.plus + self.sent + dz
            else:
                place[2, dz] = self.minus + self.sent + (self.ring - dz) - 1
        return place.reshape(-1)


def exchange_kernel(
    slots, heads, res_rows,
    tab, pair_rows, len_nodes, len_res, child_src, child_which,
    ssm, conv, comb, kv_nodes, kv_res, gather, shift, bias, unpack,
    arr, carr, att,
    gz, sp, sm, oc, cgz, csp, csm, coc, q_out, q_in, o_out, o_in,
    zsend, zrecv, xsend, xrecv, fsend, frecv, osem,
    czsend, czrecv, cxsend, cxrecv, cfsend, cfrecv, cosem,
    qsend, qrecv, rsend, rrecv,
):
    ring, half = slots.ring, slots.half
    devices = COLUMNS * ring
    me = lax.axis_index("dp")
    tensor = lax.axis_index("tensor")
    x, z = me // ring, me % ring

    def at(column, row):
        return ((column + COLUMNS) % COLUMNS) * ring + (row + ring) % ring

    above, below = at(x, z + 1), at(x, z - 1)
    right, left = at(x + 1, z), at(x - 1, z)
    across = at(x + 2, z)

    barrier = pltpu.get_barrier_semaphore()

    @pl.loop(1, devices)
    def _(step):
        pl.semaphore_signal(
            barrier, inc=1, device_id=((me + step) % devices, tensor), device_id_type=MESH
        )

    pl.semaphore_wait(barrier, devices - 1)

    def send(source, target, send_sem, recv_sem, device):
        return pltpu.make_async_remote_copy(
            src_ref=source,
            dst_ref=target,
            send_sem=send_sem,
            recv_sem=recv_sem,
            device_id=(device, tensor),
            device_id_type=MESH,
        )

    class Stream:
        def __init__(self, own, gz, sp, sm, oc, arr, zsend, zrecv, xsend, xrecv, fsend, frecv, osem):
            self.own, self.gz, self.sp, self.sm, self.oc, self.arr = own, gz, sp, sm, oc, arr
            self.zsend, self.zrecv, self.xsend, self.xrecv = zsend, zrecv, xsend, xrecv
            self.fsend, self.frecv, self.osem = fsend, frecv, osem

        def hop(self, c, k, up):
            if k == 1:
                source = self.own.at[:, c]
            else:
                source = self.gz.at[c, (ring - k + 1 if up else k - 1) - 1]
            target = self.gz.at[c, (ring - k if up else k) - 1]
            if k == half:
                nodes = pl.ds(0 if up else NODE_DEV // 2, NODE_DEV // 2)
                source, target = source.at[nodes], target.at[nodes]
            way = 0 if up else 1
            return send(
                source, target, self.zsend.at[c, way, k - 1], self.zrecv.at[c, way, k - 1],
                above if up else below,
            )

        def across_x(self, c, k, plus):
            start, size = (slots.plus_group if plus else slots.minus_group)[k]
            base = slots.plus if plus else slots.minus
            way = 0 if plus else 1
            return send(
                (self.sp if plus else self.sm).at[c, pl.ds(start, size)],
                self.arr.at[c, pl.ds(base + start, size)],
                self.xsend.at[c, way, k], self.xrecv.at[c, way, k],
                right if plus else left,
            )

        def forward(self, c, k, plus):
            if plus:
                source = slots.plus + slots.plus_transit[k]
                target = slots.plus + slots.sent + k
                index = k
            else:
                source = slots.minus + slots.minus_transit[half if k == half else ring - k]
                target = slots.minus + slots.sent + k - 1
                index = k - 1
            way = 0 if plus else 1
            return send(
                self.arr.at[c, source], self.arr.at[c, target],
                self.fsend.at[c, way, index], self.frecv.at[c, way, index],
                right if plus else left,
            )

        def own_copy(self, c):
            return pltpu.make_async_copy(
                self.oc.at[c], self.arr.at[c, pl.ds(0, ring)], self.osem.at[c]
            )

        def pick(self, c, dz, target):
            node = tab[target * devices + at(x, z + dz)]
            if dz == 0:
                return self.own[node, c]
            picked = self.gz[c, dz - 1, 0]
            for other in range(1, NODE_DEV):
                picked = jnp.where(node == other, self.gz[c, dz - 1, other], picked)
            return picked

        def group(self, c, k):
            rows = [0] if k == 0 else [half] if k == half else [k, ring - k]
            for dz in rows:
                self.sp[c, slots.plus_direct[dz]] = self.pick(c, dz, right)
                self.sm[c, slots.minus_direct[dz]] = self.pick(c, dz, left)
                if dz in slots.plus_transit:
                    self.sp[c, slots.plus_transit[dz]] = self.pick(c, dz, across)
                else:
                    self.sm[c, slots.minus_transit[dz]] = self.pick(c, dz, across)
            self.across_x(c, k, True).start()
            self.across_x(c, k, False).start()
            for dz in rows:
                self.oc[c, dz] = self.pick(c, dz, me)
            if k == half:
                self.own_copy(c).start()

        def stage(self, c, k):
            for up in (True, False):
                if k >= 1:
                    self.hop(c, k, up).wait_recv()
                if k < half:
                    self.hop(c, k + 1, up).start()
            self.group(c, k)

        def relay(self, c, k):
            for plus in (True, False):
                self.across_x(c, k, plus).wait_recv()
                if k in (range(half) if plus else range(1, half + 1)):
                    self.forward(c, k, plus).start()

        def finish(self, c):
            for k in range(1, half + 1):
                for up in (True, False):
                    self.hop(c, k, up).wait_send()
            for k in range(half + 1):
                for plus in (True, False):
                    self.across_x(c, k, plus).wait_send()
                    if k in (range(half) if plus else range(1, half + 1)):
                        self.forward(c, k, plus).wait()
            self.own_copy(c).wait()

    main = Stream(ssm, gz, sp, sm, oc, arr, zsend, zrecv, xsend, xrecv, fsend, frecv, osem)
    side = Stream(
        conv, cgz, csp, csm, coc, carr,
        czsend, czrecv, cxsend, cxrecv, cfsend, cfrecv, cosem,
    )

    def dot(a, b, dims):
        return lax.dot_general(a, b, (dims, ((), ())), preferred_element_type=jnp.float32)

    def weigh(weights, values):
        high = weights.astype(jnp.bfloat16)
        low = (weights - high.astype(jnp.float32)).astype(jnp.bfloat16)
        return dot(high, values, ((1,), (0,))) + dot(low, values, ((1,), (0,)))

    def attend(message, keys, values, length):
        scale = HEAD**-0.5
        old = dot(message, keys, ((1,), (1,))) * scale
        spot = lax.broadcasted_iota(jnp.int32, old.shape, 1)
        old = jnp.where(spot < length, old, -jnp.inf)
        moved = dot(shift[...], message, ((1,), (0,))).astype(jnp.bfloat16)
        new = dot(message, moved, ((1,), (1,))) * scale + bias[...]
        top = jnp.maximum(jnp.max(old, 1, keepdims=True), jnp.max(new, 1, keepdims=True))
        old, new = jnp.exp(old - top), jnp.exp(new - top)
        total = jnp.sum(old, 1, keepdims=True) + jnp.sum(new, 1, keepdims=True)
        return (weigh(old, values) + weigh(new, message)) / total

    def pack(first, second):
        both = jnp.concatenate([comb[first], comb[second]], 0)
        return dot(gather[...], both, ((1,), (0,))).astype(jnp.bfloat16)

    def ask(d):
        return send(q_out.at[d], q_in.at[me], qsend.at[d], qrecv.at[me], d)

    def asked(d):
        return send(q_out.at[d], q_in.at[d], qsend.at[d], qrecv.at[d], d)

    def reply(d):
        return send(o_out.at[d], o_in.at[me], rsend.at[d], rrecv.at[me], d)

    def replied(d):
        return send(o_out.at[d], o_in.at[d], rsend.at[d], rrecv.at[d], d)

    def ask_all():
        @pl.loop(0, devices)
        def _(step):
            d = (me + step) % devices
            message = pack(res_rows + pair_rows[d], res_rows + pair_rows[devices + d])

            @pl.when(step == 0)
            def _():
                q_in[me] = message

            @pl.when(step != 0)
            def _():
                q_out[d] = message
                ask(d).start()

    def serve(step):
        d = (me + devices - step) % devices

        @pl.when(step != 0)
        def _():
            asked(d).wait_recv()

        node = tab[d * devices + me]
        result = attend(q_in[d], kv_nodes[node, 0], kv_nodes[node, 1], len_nodes[me * NODE_DEV + node])
        result = result[:BACK].astype(jnp.bfloat16)

        @pl.when(step == 0)
        def _():
            o_in[me] = result

        @pl.when(step != 0)
        def _():
            o_out[d] = result
            reply(d).start()

    def resident(row):
        result = attend(pack(row, row), kv_res[row, 0], kv_res[row, 1], len_res[row])
        att[row] = result[:BLOCK].astype(jnp.bfloat16)

    batch = 4
    begin = [0] + [k + 1 for k in range(1, half + 1)]

    @pl.loop(0, heads + half + 2)
    def _(tick):
        for k in range(half, -1, -1):
            c = tick - begin[k]

            @pl.when(c == 0)
            def _():
                side.stage(0, k)

            @pl.when((c >= 0) & (c < heads))
            def _():
                main.stage(c, k)

        for k in range(half, -1, -1):
            c = tick - begin[k] - 1

            @pl.when(c == 0)
            def _():
                side.relay(0, k)

            @pl.when((c >= 0) & (c < heads))
            def _():
                main.relay(c, k)

        @pl.when(tick == 0)
        def _():
            ask_all()

        @pl.when(tick == 1)
        def _():
            @pl.loop(0, res_rows)
            def _(row):
                resident(row)

        @pl.when((tick >= 2) & (tick < 2 + devices // batch))
        def _():
            @pl.loop(0, batch)
            def _(i):
                serve((tick - 2) * batch + i)

    @pl.loop(1, devices)
    def _(step):
        d = (me + step) % devices
        replied(d).wait_recv()

    @pl.loop(0, child_src.shape[0])
    def _(child):
        mine = jnp.where(child_which[child] == 1, unpack[1], unpack[0])
        att[res_rows + child] = dot(mine, o_in[child_src[child]], ((1,), (0,))).astype(jnp.bfloat16)

    side.finish(0)

    @pl.loop(0, heads)
    def _(c):
        main.finish(c)

    @pl.loop(1, devices)
    def _(step):
        d = (me + step) % devices
        ask(d).wait_send()
        reply(d).wait_send()


def exchange(tab, pair_rows, len_nodes, len_res, child_src, child_which, ssm, conv, comb, kv_nodes, kv_res, ring):
    slots = Slots(ring)
    half = ring // 2
    devices = COLUMNS * ring
    heads = ssm.shape[1]
    rows = comb.shape[0]
    gather, shift, bias, unpack = pair_constants()
    smem = pl.BlockSpec(memory_space=pltpu.SMEM)
    vmem = pl.BlockSpec(memory_space=pltpu.VMEM)
    anywhere = pl.BlockSpec(memory_space=pl.ANY)
    bf16 = jnp.bfloat16

    def buffers(count, height):
        return [
            pltpu.VMEM((count, ring - 1, NODE_DEV, height, STATE), bf16),
            pltpu.VMEM((count, slots.sent, height, STATE), bf16),
            pltpu.VMEM((count, slots.sent, height, STATE), bf16),
            pltpu.VMEM((count, ring, height, STATE), bf16),
        ]

    def semaphores(count):
        dma = pltpu.SemaphoreType.DMA
        return [
            dma((count, 2, half)), dma((count, 2, half)),
            dma((count, 2, half + 1)), dma((count, 2, half + 1)),
            dma((count, 2, half)), dma((count, 2, half)),
            dma((count,)),
        ]

    return pl.pallas_call(
        functools.partial(exchange_kernel, slots, heads, kv_res.shape[0]),
        out_shape=[
            jax.ShapeDtypeStruct((heads, slots.total, SSM_HEAD, STATE), bf16),
            jax.ShapeDtypeStruct((1, slots.total, 16, STATE), bf16),
            jax.ShapeDtypeStruct((rows, BLOCK, HEAD), bf16),
        ],
        in_specs=[smem] * 6 + [vmem] * 9,
        out_specs=[anywhere, anywhere, vmem],
        scratch_shapes=buffers(heads, SSM_HEAD)
        + buffers(1, 16)
        + [
            pltpu.VMEM((devices, PAIR, HEAD), bf16),
            pltpu.VMEM((devices, PAIR, HEAD), bf16),
            pltpu.VMEM((devices, BACK, HEAD), bf16),
            pltpu.VMEM((devices, BACK, HEAD), bf16),
        ]
        + semaphores(heads)
        + semaphores(1)
        + [pltpu.SemaphoreType.DMA((devices,))] * 4,
        compiler_params=pltpu.CompilerParams(
            collective_id=0, has_side_effects=True, vmem_limit_bytes=40 * 1024 * 1024
        ),
        name="exchange",
    )(
        tab, pair_rows, len_nodes, len_res, child_src, child_which,
        ssm, conv, comb, kv_nodes, kv_res,
        jnp.asarray(gather, bf16), jnp.asarray(shift, bf16), jnp.asarray(bias), jnp.asarray(unpack, bf16),
    )


def state_kernel(res_rows, place, last_decay, res, arr, c_parts, b_parts, w_parts, new_ssm, read):
    row = pl.program_id(0)
    heads = res.shape[1]

    def work(state):
        sums = lax.dot_general(
            c_parts[0], state, (((1,), (1,)), ((), ())), preferred_element_type=jnp.float32
        )
        read[0] = sums[0:4] + sums[4:8] + sums[8:12]
        added = lax.dot_general(
            w_parts[0], b_parts[0], (((0,), (0,)), ((), ())), preferred_element_type=jnp.float32
        )
        for h in range(heads):
            span = slice(h * SSM_HEAD, (h + 1) * SSM_HEAD)
            new = last_decay[row * heads + h] * state[span].astype(jnp.float32) + added[span]
            new_ssm[0, h] = new.astype(jnp.bfloat16)

    @pl.when(row < res_rows)
    def _():
        work(res[0].reshape(heads * SSM_HEAD, STATE))

    @pl.when(row >= res_rows)
    def _():
        work(arr[:, 0].reshape(heads * SSM_HEAD, STATE))


def update_states(place, last_decay, res, arr, c_parts, b_parts, w_parts):
    res_rows, heads = res.shape[:2]
    rows = c_parts.shape[0]
    features = heads * SSM_HEAD

    def by_row(shape):
        return pl.BlockSpec((1,) + shape, lambda r, p, d: (r,) + (0,) * len(shape))

    return pl.pallas_call(
        functools.partial(state_kernel, res_rows),
        out_shape=[
            jax.ShapeDtypeStruct((rows, heads, SSM_HEAD, STATE), jnp.bfloat16),
            jax.ShapeDtypeStruct((rows, STEPS, features), jnp.float32),
        ],
        grid_spec=pltpu.PrefetchScalarGridSpec(
            num_scalar_prefetch=2,
            grid=(rows,),
            in_specs=[
                pl.BlockSpec(
                    (1, heads, SSM_HEAD, STATE), lambda r, p, d: (jnp.minimum(r, res_rows - 1), 0, 0, 0)
                ),
                pl.BlockSpec((heads, 1, SSM_HEAD, STATE), lambda r, p, d: (0, p[r], 0, 0)),
                by_row((16, STATE)),
                by_row((16, STATE)),
                by_row((16, features)),
            ],
            out_specs=[by_row((heads, SSM_HEAD, STATE)), by_row((STEPS, features))],
        ),
        name="states",
    )(place, last_decay, res, arr, c_parts, b_parts, w_parts)


def norm_kernel(peers, read, decay, rest, gate, gain, alive, out, sums, landed, send_sem, recv_sem):
    me = lax.axis_index("tensor")
    dp = lax.axis_index("dp")
    if peers > 1:
        barrier = pltpu.get_barrier_semaphore()

        @pl.loop(1, peers)
        def _(step):
            pl.semaphore_signal(
                barrier, inc=1, device_id=(dp, (me + step) % peers), device_id_type=MESH
            )

    gated = (read[...] * decay[...] + rest[...]) * jax.nn.silu(gate[...].astype(jnp.float32))
    total = lax.dot_general(
        jnp.ones((8, gated.shape[1]), jnp.float32), gated * gated, (((1,), (1,)), ((), ())),
        precision=HIGHEST, preferred_element_type=jnp.float32,
    )
    sums[...] = total

    def copy(d, slot):
        return pltpu.make_async_remote_copy(
            src_ref=sums, dst_ref=landed.at[slot], send_sem=send_sem.at[d], recv_sem=recv_sem.at[slot],
            device_id=(dp, d), device_id_type=MESH,
        )

    if peers > 1:
        pl.semaphore_wait(barrier, peers - 1)

        @pl.loop(1, peers)
        def _(step):
            copy((me + step) % peers, me).start()

        @pl.loop(1, peers)
        def _(step):
            d = (me + step) % peers
            copy(d, d).wait_recv()

        landed[me] = sums[...]
        total = landed[0]
        for d in range(1, peers):
            total = total + landed[d]
    scale = lax.rsqrt(total / INNER + EPSILON)
    first = lax.broadcasted_iota(jnp.int32, scale.shape, 0) == 0
    column = lax.dot_general(
        jnp.where(first, scale, 0.0), jnp.ones((8, 128), jnp.float32), (((0,), (0,)), ((), ())),
        precision=HIGHEST, preferred_element_type=jnp.float32,
    )
    result = gated * column[:, 0:1] * gain[...]
    out[...] = jnp.where(alive[...] > 0, result, 0.0).astype(jnp.bfloat16)
    if peers > 1:

        @pl.loop(1, peers)
        def _(step):
            copy((me + step) % peers, me).wait_send()


def gated_norm(read, decay, rest, gate, gain, alive, peers):
    lines, features = read.shape
    return pl.pallas_call(
        functools.partial(norm_kernel, peers),
        out_shape=jax.ShapeDtypeStruct((lines, features), jnp.bfloat16),
        in_specs=[pl.BlockSpec(memory_space=pltpu.VMEM)] * 6,
        out_specs=pl.BlockSpec(memory_space=pltpu.VMEM),
        scratch_shapes=[
            pltpu.VMEM((8, lines), jnp.float32),
            pltpu.VMEM((peers, 8, lines), jnp.float32),
            pltpu.SemaphoreType.DMA((peers,)),
            pltpu.SemaphoreType.DMA((peers,)),
        ],
        compiler_params=pltpu.CompilerParams(collective_id=1 if peers > 1 else None, has_side_effects=True),
        name="norm",
    )(read, decay, rest, gate, gain, alive)


def split(value, parts):
    pieces = []
    for _ in range(parts):
        piece = lax.reduce_precision(value, 8, 7)
        pieces.append(piece.astype(jnp.bfloat16))
        value = value - piece
    return pieces


def per_device(
    ssm_resident, ssm_nodes, conv_resident, conv_nodes, convbc_resident, convbc_nodes,
    kv_resident, kv_nodes, len_resident, len_nodes, parents, alive_flags, queries, new_kv,
    x_in, gate_in, bc_in, dt_in, conv_x_weight, conv_bc_weight, a_log, dt_bias, skip_gain, norm_gain,
):
    devices = lax.axis_size("dp")
    peers = lax.axis_size("tensor")
    me = lax.axis_index("dp")
    ring = devices // COLUMNS
    child_dev = parents.shape[0] // devices
    rows = queries.shape[0]
    res_rows = ssm_resident.shape[0]
    heads = ssm_nodes.shape[1]
    features = heads * SSM_HEAD
    bf16, f32 = jnp.bfloat16, jnp.float32

    grouped = parents.reshape(devices, child_dev)
    match = (grouped // NODE_DEV)[:, None, :] == jnp.arange(devices)[None, :, None]
    tab = jnp.max(jnp.where(match, (grouped % NODE_DEV)[:, None, :], 0), axis=2).reshape(-1)
    own = lax.dynamic_slice_in_dim(parents, me * child_dev, child_dev)
    child_src = own // NODE_DEV
    mine = child_src[None, :] == jnp.arange(devices)[:, None]
    number = jnp.arange(child_dev)[None, :]
    first = jnp.min(jnp.where(mine, number, child_dev - 1), axis=1)
    second = jnp.max(jnp.where(mine, number, 0), axis=1)
    child_which = jnp.sum(jnp.where(mine & (number > first[:, None]), 1, 0), axis=0)
    relative = (
        (child_src // ring - me // ring) % COLUMNS * ring + (child_src % ring - me % ring) % ring
    )
    place = jnp.take(jnp.asarray(Slots(ring).table()), relative)

    convs = conv_nodes.reshape(NODE_DEV, -1, STATE)
    convbcs = convbc_nodes.reshape(NODE_DEV, -1, STATE)
    used = convs.shape[1]
    convp = jnp.concatenate(
        [convs, convbcs, jnp.zeros((NODE_DEV, 16 - used - 6, STATE), bf16)], 1
    )[:, None]
    comb = jnp.concatenate(
        [
            queries.reshape(rows, STEPS, GROUP, HEAD).transpose(0, 2, 1, 3).reshape(rows, 20, HEAD),
            new_kv.reshape(rows, 2 * STEPS, HEAD),
            jnp.zeros((rows, 4, HEAD), bf16),
        ],
        1,
    )
    arr, carr, att = exchange(
        tab, jnp.concatenate([first, second]), len_nodes, len_resident, child_src, child_which,
        ssm_nodes, convp, comb, kv_nodes, kv_resident, ring,
    )

    got = jnp.take(carr[0], place, axis=0)
    all_conv = jnp.concatenate([conv_resident, got[:, :used].reshape(child_dev, KERNEL - 1, -1)], 0)
    all_convbc = jnp.concatenate(
        [convbc_resident, got[:, used : used + 6].reshape(child_dev, KERNEL - 1, -1)], 0
    )
    conv_input = jnp.concatenate([all_conv, x_in], 1).astype(f32)
    conv_bc_input = jnp.concatenate([all_convbc, bc_in], 1).astype(f32)
    mixed_x = jnp.zeros(x_in.shape, f32)
    mixed_bc = jnp.zeros(bc_in.shape, f32)
    for tap in range(KERNEL):
        mixed_x = mixed_x + conv_x_weight[tap].astype(f32) * conv_input[:, tap : tap + STEPS]
        mixed_bc = mixed_bc + conv_bc_weight[tap].astype(f32) * conv_bc_input[:, tap : tap + STEPS]
    mixed_x = jax.nn.silu(mixed_x)
    mixed_bc = jax.nn.silu(mixed_bc)
    b_part = mixed_bc[:, :, :STATE]
    c_part = mixed_bc[:, :, STATE:]
    dt = jax.nn.softplus(dt_in.astype(f32) + dt_bias)
    decay = jnp.exp(-jnp.exp(a_log) * dt)

    def spread(value):
        return jnp.repeat(value, SSM_HEAD, axis=-1)

    rest, since = [], []
    scaled = [spread(dt[:, t]) * mixed_x[:, t] for t in range(STEPS)]
    carried = []
    for t in range(STEPS):
        step_decay = decay[:, t]
        since = [d * step_decay for d in since] + [jnp.ones_like(step_decay)]
        carried.append(step_decay if t == 0 else carried[-1] * step_decay)
        value = spread(skip_gain) * mixed_x[:, t]
        for s in range(t + 1):
            overlap = jnp.sum(c_part[:, t] * b_part[:, s], -1, keepdims=True)
            value = value + spread(since[s]) * overlap * scaled[s]
        rest.append(value)
    rest = jnp.stack(rest, 1)
    carried = jnp.stack(carried, 1)
    weights = jnp.stack([spread(since[s]) * scaled[s] for s in range(STEPS)], 1)

    def padded(pieces):
        return jnp.concatenate(pieces + [jnp.zeros_like(pieces[0])], 1)

    c_parts = padded(split(c_part, 3))
    b_high, b_low = split(b_part, 2)
    w_high, w_low = split(weights, 2)
    b_parts = padded([b_high, b_low, b_high])
    w_parts = padded([w_high, w_high, w_low])
    place_all = jnp.concatenate([jnp.broadcast_to(place[0], (res_rows,)), place])
    new_ssm, read = update_states(
        place_all, carried[:, -1].reshape(-1), ssm_resident, arr, c_parts, b_parts, w_parts
    )
    lines = rows * STEPS
    alive = jnp.repeat(alive_flags, STEPS)[:, None]
    ssm_out = gated_norm(
        read.reshape(lines, features),
        spread(carried).reshape(lines, features),
        rest.reshape(lines, features),
        gate_in.reshape(lines, features),
        norm_gain[None, :],
        alive,
        peers,
    ).reshape(rows, STEPS, features)
    attn = att[:, :20].reshape(rows, GROUP, STEPS, HEAD).transpose(0, 2, 1, 3).reshape(rows, STEPS, -1)
    attn = jnp.where((alive_flags > 0)[:, None, None], attn, jnp.zeros((), bf16))
    return attn, ssm_out, new_ssm


def solution(mesh):
    return jax.shard_map(
        per_device,
        mesh=mesh,
        in_specs=(
            P("dp", "tensor", None, None),
            P("dp", "tensor", None, None),
            P("dp", None, "tensor"),
            P("dp", None, "tensor"),
            P("dp", None, None),
            P("dp", None, None),
            P("dp", None, None, "tensor"),
            P("dp", None, None, "tensor"),
            P("dp"),
            P(),
            P(),
            P("dp"),
            P("dp", None, "tensor"),
            P("dp", None, None, "tensor"),
            P("dp", None, "tensor"),
            P("dp", None, "tensor"),
            P("dp", None, None),
            P("dp", None, "tensor"),
            P(None, "tensor"),
            P(),
            P("tensor"),
            P("tensor"),
            P("tensor"),
            P("tensor"),
        ),
        out_specs=(P("dp", None, "tensor"), P("dp", None, "tensor"), P("dp", "tensor", None, None)),
        check_vma=False,
    )
```

time: 435 us -> 203 us (0.47)
  waiting for transfers between devices: 251 us -> 0 us
  Pallas kernels: 0 us -> 164 us
  matrix products: 71.2 us -> 0 us
  starting transfers between devices: 29.2 us -> 0 us
  other arithmetic: 34.5 us -> 8.03 us
  blocking collectives: 15.7 us -> 0 us
    all_to_all x4 -> x0, waiting for transfers between devices: 251 us -> none  [the longest x1 162 us: per_device(): lax.all_to_all(pack_nodes(ssm_nodes), 'dp', split_axis=0, concat_axis=0,...]
    pallas_call x0 -> x3, Pallas kernels: none -> 164 us  [the longest x1 135 us: exchange(): pl.pallas_call(functools.partial(exchange_kernel, slots, heads, kv_res.sh...]
    dot_general x8 -> x0, matrix products: 71.2 us -> none  [the longest x4 66 us: per_device(): jnp.einsum('rhpn,rn->rhp', carry_state, c_part[:, t], precision=lax.Preci...]
    all_to_all x4 -> x0, starting transfers between devices: 29.2 us -> none  [the longest x1 11.9 us: per_device(): lax.all_to_all(pack_nodes(conv_nodes), 'dp', split_axis=0, concat_axis=0,...]
    gather x9 -> x2, local copies, waits for them, and re-layouts: 23.5 us -> 1.21 us  [the longest x1 0.66 us: per_device(): place = jnp.take(jnp.asarray(Slots(ring).table()), relative)]
    psum x1 -> x0, blocking collectives: 15.7 us -> none  [per_device(): square_sums = lax.psum(jnp.sum(gated_out * gated_out, -1), 'tensor')]
    select_n x8 -> x6, other arithmetic: 16.3 us -> 1.07 us  [the longest x1 0.78 us: per_device(): place = jnp.take(jnp.asarray(Slots(ring).table()), relative)]
    unnamed x82 -> x52, local copies, waits for them, and re-layouts: 1.6 us -> 14.8 us
  transfers between devices with their start and end apart: 4 -> 0, of which waited for: 4 -> 0; matrix products, arithmetic and copies ran while one was open for 10% -> 0% of each run, Pallas kernels for 0% -> 0%
where the time goes in v1:
time: 203 us; the launch traced here: 201 us
  Pallas kernels  164 us (81%)
  local copies, waits for them, and re-layouts  28.2 us (14%)
  other arithmetic  8.03 us (4%)
    pallas_call x1, Pallas kernels, exchange(): pl.pallas_call(functools.partial(exchange_kernel, slots, heads, kv_res.sh...  135 us
    pallas_call x1, Pallas kernels, update_states(): pl.pallas_call(functools.partial(state_kernel, res_rows), out_shape=[jax....  18.7 us
    unnamed x52, local copies, waits for them, and re-layouts  14.8 us
    pallas_call x1, Pallas kernels, gated_norm(): pl.pallas_call(functools.partial(norm_kernel, peers), out_shape=jax.Shape...  10.5 us

profile of v1, /device:TPU:1, one launch (start us, length us, event | category | flops | bytes accessed | tf_op | source)
XLA Modules:
  0.0 201.4 jit_solution(8934951016695317055)
XLA Ops:
  0.7 0.9 reshape.464
  1.6 0.2 select_reduce_fusion
  1.9 0.8 compare_select_fusion.2
  2.8 0.1 select_reduce_fusion.1
  3.0 0.7 copy.97
  3.8 0.7 copy.96
  4.7 0.9 copy.98
  5.6 0.2 reshape.468
  5.9 0.9 maximum_maximum_fusion.1.comb
  6.8 1.2 copy-done.1
  8.0 1.2 copy-done.2
  9.3 1.0 copy-done.3
  10.3 0.8 copy-done.4
  11.1 0.7 copy-done.5
  11.8 0.7 copy-done.6
  12.5 0.7 copy-done.7
  13.2 0.7 copy-done.8
  13.9 0.7 copy-done.9
  14.5 134.7 %exchange.1 = (bf16[8,40,64,256]{3,2,1,0:T(8,128)(2,1)S(1)}, bf16[1,40,16,256]{3,2,1,0:T(8,128)(2,1)S(1)}, bf16[24,32,128]{2,1,0:T(8,128)(2,1)S(1)}) custom-call(s32[1024]{0:T(1024)S(1)} %reshape.465.tab, s32[64]{0:T(128)S(1)} %pad_add_fusion.pair_rows, s32[128]{0:T(128)S(1)} %copy-done.8, s32[8]{0:T(128)S(1)} %copy-done.9, ...), custom_call_target="tpu_custom_call" | custom-call | tf_op jit(solution)/shard_map/exchange/pallas_call | solution.py:407
  149.3 4.0 %copy-done = bf16[8,40,64,256]{3,2,1,0:T(8,128)(2,1)} copy-done((bf16[8,40,64,256]{3,2,1,0:T(8,128)(2,1)}, bf16[8,40,64,256]{3,2,1,0:T(8,128)(2,1)S(1)}, u32[]{:S(2)}) %copy-start) | copy-done | bytes 10485784
  153.3 0.7 broadcast_compare_fusion
  154.0 0.7 copy.118
  154.7 0.7 gather_fusion
  155.4 0.6 concatenate.36.place
  156.3 0.7 mul.384.last_decay
  156.9 0.6 gather_fusion.1
  157.9 0.2 divide_multiply_fusion.1
  158.2 1.0 maximum_maximum_fusion.3
  159.7 0.2 divide_multiply_fusion
  160.0 0.7 fusion.12
  161.0 0.1 reshape.475
  161.7 0.1 reshape.478
  161.8 0.2 multiply_add_fusion.2
  162.2 0.1 reshape.477
  162.4 0.1 reshape.474
  163.1 0.4 multiply_add_fusion
  164.1 0.2 multiply_add_fusion.1
  164.3 0.4 reduce-precision_convert_fusion
  164.7 1.0 maximum_maximum_fusion.w_parts
  165.7 18.7 %states.1 = (bf16[24,8,64,256]{3,2,1,0:T(8,128)(2,1)}, f32[24,4,512]{2,1,0:T(4,128)}) custom-call(s32[24]{0:T(128)} %concatenate.36.place, f32[192]{0:T(256)} %mul.384.last_decay, bf16[8,8,64,256]{3,2,1,0:T(8,128)(2,1)} %res.1, bf16[8,40,64,256]{3,2,1,0:T(8,128)(2,1)} %copy-done, bf16[24,16,256]{2,1,0:T(8,128)(2,1)} %get-tuple-element.86.c_parts, ...), custom_call_target="tpu_custom_call" | custom-call | tf_op jit(solution)/shard_map/states/pallas_call | solution.py:472
  184.4 1.7 reshape.482.read
  186.1 0.2 broadcast_in_dim.173
  186.3 0.8 reshape_reshape.3.decay
  187.1 0.7 reshape.486.rest
  187.9 0.7 reshape.487.gate
  188.6 0.7 broadcast_in_dim_reshape.3.alive
  189.3 10.5 %norm.1 = bf16[96,512]{1,0:T(8,128)(2,1)} custom-call(f32[96,512]{1,0:T(8,128)} %reshape.482.read, f32[96,512]{1,0:T(8,128)} %reshape_reshape.3.decay, f32[96,512]{1,0:T(8,128)} %reshape.486.rest, bf16[96,512]{1,0:T(8,128)(2,1)} %reshape.487.gate, f32[1,512]{1,0:T(1,128)} %bitcast.68, s32[96,1]{1,0:T(8,128)} %broadcast_in_dim_reshape.3.alive), custom_call_target="tpu_custom_call" | custom-call | tf_op jit(solution)/shard_map/norm/pallas_call | solution.py:554
  199.8 1.6 reshape.488
  (104 shorter events, 4.2 us)
Async XLA Ops:
  0.6 154.1 %copy-start.10 = (s32[32]{0:T(128)S(1)}, s32[32]{0:T(128)}, u32[]{:S(2)}) copy-start(s32[32]{0:T(128)} %constant.157.clone) | copy-start | bytes 388
  0.6 155.4 %copy-start.18 = (bf16[24,4,8]{0,2,1:T(8,128)(2,1)S(1)}, bf16[24,4,8]{0,2,1:T(8,128)(2,1)}, u32[]{:S(2)}) copy-start(bf16[24,4,8]{0,2,1:T(8,128)(2,1)} %param.46) | copy-start | bytes 4612
  0.7 155.4 %copy-start.19 = (f32[8]{0:T(128)S(1)}, f32[8]{0:T(128)}, u32[]{:S(2)}) copy-start(f32[8]{0:T(128)} %param.50) | copy-start | bytes 100
  0.7 155.4 %copy-start.22 = (f32[8]{0:T(128)S(1)}, f32[8]{0:T(128)}, u32[]{:S(2)}) copy-start(f32[8]{0:T(128)} %param.49) | copy-start | bytes 100
  0.7 157.0 %copy-start.11 = (bf16[24,4,512]{2,1,0:T(4,128)(2,1)S(1)}, bf16[24,4,512]{2,1,0:T(4,128)(2,1)}, u32[]{:S(2)}) copy-start(bf16[24,4,512]{2,1,0:T(4,128)(2,1)} %param.45) | copy-start | bytes 294916
  0.7 157.0 %copy-start.14 = (bf16[8,3,512]{2,0,1:T(8,128)(2,1)S(1)}, bf16[8,3,512]{2,0,1:T(8,128)(2,1)}, u32[]{:S(2)}) copy-start(bf16[8,3,512]{2,0,1:T(8,128)(2,1)} %param.33) | copy-start | bytes 73732
  0.7 157.1 %copy-start.16 = (bf16[4,512]{1,0:T(4,128)(2,1)S(1)}, bf16[4,512]{1,0:T(4,128)(2,1)}, u32[]{:S(2)}) copy-start(bf16[4,512]{1,0:T(4,128)(2,1)} %param.48) | copy-start | bytes 12292
  0.7 158.9 %copy-start.12 = (bf16[24,4,512]{2,1,0:T(4,128)(2,1)S(1)}, bf16[24,4,512]{2,1,0:T(4,128)(2,1)}, u32[]{:S(2)}) copy-start(bf16[24,4,512]{2,1,0:T(4,128)(2,1)} %param.43) | copy-start | bytes 294916
  0.7 158.8 %copy-start.15 = (bf16[8,3,512]{2,0,1:T(8,128)(2,1)S(1)}, bf16[8,3,512]{2,0,1:T(8,128)(2,1)}, u32[]{:S(2)}) copy-start(bf16[8,3,512]{2,0,1:T(8,128)(2,1)} %param.31) | copy-start | bytes 73732
  0.7 159.0 %copy-start.17 = (bf16[4,512]{1,0:T(4,128)(2,1)S(1)}, bf16[4,512]{1,0:T(4,128)(2,1)}, u32[]{:S(2)}) copy-start(bf16[4,512]{1,0:T(4,128)(2,1)} %param.47) | copy-start | bytes 12292
  1.6 159.1 %copy-start.20 = (f32[8]{0:T(128)S(1)}, f32[8]{0:T(128)}, u32[]{:S(2)}) copy-start(f32[8]{0:T(128)} %param.51) | copy-start | bytes 100
  6.8 1.2 copy-start.1
  8.0 1.2 copy-start.2
  9.3 1.0 copy-start.3
  10.3 0.8 copy-start.4
  11.1 0.7 copy-start.5
  11.8 0.7 copy-start.6
  12.5 0.7 copy-start.7
  13.2 0.7 copy-start.8
  13.9 0.7 copy-start.9
  149.3 4.0 %copy-start = (bf16[8,40,64,256]{3,2,1,0:T(8,128)(2,1)}, bf16[8,40,64,256]{3,2,1,0:T(8,128)(2,1)S(1)}, u32[]{:S(2)}) copy-start(bf16[8,40,64,256]{3,2,1,0:T(8,128)(2,1)S(1)} %get-tuple-element.9.arr) | copy-start | bytes 31457284
  165.7 22.2 %copy-start.13 = (bf16[24,4,512]{2,1,0:T(4,128)(2,1)S(1)}, bf16[24,4,512]{2,1,0:T(4,128)(2,1)}, u32[]{:S(2)}) copy-start(bf16[24,4,512]{2,1,0:T(4,128)(2,1)} %param.44) | copy-start | bytes 294916
  165.7 22.8 %copy-start.21 = (s32[24]{0:T(128)S(1)}, s32[24]{0:T(128)}, u32[]{:S(2)}) copy-start(s32[24]{0:T(128)} %param.40) | copy-start | bytes 292

commit v2 on v1

v2 whole, which is shorter than its diff:
```python
import functools

import jax
import jax.numpy as jnp
import numpy as np
from jax import lax
from jax.experimental import pallas as pl
from jax.experimental.pallas import tpu as pltpu
from jax.sharding import PartitionSpec as P

HEAD = 128
SSM_HEAD = 64
STATE = 256
KERNEL = 4
STEPS = 4
INNER = 4096
EPSILON = 1e-05
NODE_DEV = 4
GROUP = 5
COLUMNS = 4
MESH = pl.DeviceIdType.MESH


class Slots:
    def __init__(self, ring):
        half = ring // 2
        self.ring, self.half = ring, half
        self.plus_direct, self.plus_transit = {0: 0}, {0: 1}
        self.minus_direct, self.minus_transit = {0: 0}, {}
        self.plus_group, self.minus_group = [(0, 2)], [(0, 1)]
        for k in range(1, half):
            start = 2 + 3 * (k - 1)
            self.plus_direct[k], self.plus_direct[ring - k], self.plus_transit[k] = start, start + 1, start + 2
            self.plus_group.append((start, 3))
            start = 1 + 3 * (k - 1)
            self.minus_direct[k], self.minus_direct[ring - k], self.minus_transit[ring - k] = start, start + 1, start + 2
            self.minus_group.append((start, 3))
        start = 2 + 3 * (half - 1)
        self.plus_direct[half] = start
        self.plus_group.append((start, 1))
        start = 1 + 3 * (half - 1)
        self.minus_direct[half], self.minus_transit[half] = start, start + 1
        self.minus_group.append((start, 2))
        self.sent = 3 * half
        self.plus = ring
        self.minus = ring + self.sent + half
        self.total = ring + 2 * (self.sent + half)

    def table(self):
        place = np.zeros((COLUMNS, self.ring), np.int32)
        for dz in range(self.ring):
            place[0, dz] = dz
            place[3, dz] = self.plus + self.plus_direct[dz]
            place[1, dz] = self.minus + self.minus_direct[dz]
            if dz < self.half:
                place[2, dz] = self.plus + self.sent + dz
            else:
                place[2, dz] = self.minus + self.sent + (self.ring - dz) - 1
        return place.reshape(-1)


PAIR = 64
BACK = 48
BLOCK = 32
GROUPS = 2


def dot(a, b, dims):
    return lax.dot_general(a, b, (dims, ((), ())), preferred_element_type=jnp.float32)


def silu(value):
    return value / (1.0 + jnp.exp(-value))


def softplus(value):
    return jnp.maximum(value, 0.0) + jnp.log1p(jnp.exp(-jnp.abs(value)))


def split(value, parts):
    pieces = []
    for _ in range(parts):
        piece = value.astype(jnp.bfloat16).astype(jnp.float32)
        pieces.append(piece)
        value = value - piece
    return pieces


def round_kernel(
    slots, heads, res_rows, child_dev, peers,
    plan, len_nodes, len_res, alive, a_log, dt_bias, skip_gain,
    ssm_h, res_h, kvn_h, kvr_h, q_h, nkv_h, x_h, g_h, bc_h, dt_h, cr_h, cbr_h, cn_h, cbn_h, wx_h, wbc_h, gain_h,
    att, ssm_out, new_out,
    *scratch,
):
    scratch = list(scratch)

    def take(count):
        taken, scratch[:count] = scratch[:count], []
        return taken

    loaded = take(17)
    (ssm, res, kv_nodes, kv_res, q_v, nkv_v, x_v, g_v, bc_v, dt_v, cr_v, cbr_v, cn_v, cbn_v, wx_v, wbc_v, gain_v) = loaded
    (load_sem,) = take(1)
    comb, convp, new_v, gather, shift, bias = take(6)
    ux, ub, c_parts, b_parts, w_parts, carried, rest, read = take(8)
    q_out, q_in, o_out, o_in = take(4)
    qsend, qrecv, rsend, rrecv = take(4)
    sums, landed, psend, precv = take(4)
    (new_sem,) = take(1)

    ring, half = slots.ring, slots.half
    devices = COLUMNS * ring
    rows = res_rows + child_dev
    features = heads * SSM_HEAD
    me = lax.axis_index("dp")
    tensor = lax.axis_index("tensor")
    x, z = me // ring, me % ring
    first_at = devices * devices
    second_at = first_at + devices
    src_at = second_at + devices
    which_at = src_at + child_dev
    place_at = which_at + child_dev

    sources = (ssm_h, res_h, kvn_h, kvr_h, q_h, nkv_h, x_h, g_h, bc_h, dt_h, cr_h, cbr_h, cn_h, cbn_h, wx_h, wbc_h, gain_h)
    loads = [pltpu.make_async_copy(a, b, load_sem.at[i]) for i, (a, b) in enumerate(zip(sources, loaded))]
    for load in loads:
        load.start()

    barrier = pltpu.get_barrier_semaphore()

    @pl.loop(1, devices)
    def _(step):
        pl.semaphore_signal(
            barrier, inc=1, device_id=((me + step) % devices, tensor), device_id_type=MESH
        )

    if peers > 1:

        @pl.loop(1, peers)
        def _(step):
            pl.semaphore_signal(
                barrier, inc=1, device_id=(me, (tensor + step) % peers), device_id_type=MESH
            )

    for load in loads:
        load.wait()

    def at(column, row):
        return ((column + COLUMNS) % COLUMNS) * ring + (row + ring) % ring

    above, below = at(x, z + 1), at(x, z - 1)
    right, left = at(x + 1, z), at(x - 1, z)
    across = at(x + 2, z)

    for node in range(NODE_DEV):
        lines = []
        for value in (cn_v, cbn_v):
            for j in range(KERNEL - 1):
                for begin in range(0, value.shape[2], STATE):
                    lines.append(value[j].astype(jnp.float32)[node : node + 1, begin : begin + STATE])
        used = len(lines)
        lines.append(jnp.zeros((16 - used, STATE), jnp.float32))
        convp[node, 0] = jnp.concatenate(lines, 0).astype(jnp.bfloat16)
    x_lines = (KERNEL - 1) * features // STATE

    pl.semaphore_wait(barrier, devices - 1 + peers - 1)

    def send(source, target, send_sem, recv_sem, device):
        return pltpu.make_async_remote_copy(
            src_ref=source,
            dst_ref=target,
            send_sem=send_sem,
            recv_sem=recv_sem,
            device_id=(device, tensor),
            device_id_type=MESH,
        )

    class Stream:
        def __init__(self, own, base, refs):
            self.own, self.base = own, base
            (self.gz, self.sp, self.sm, self.arr,
             self.zsend, self.zrecv, self.xsend, self.xrecv, self.fsend, self.frecv) = refs

        def hop(self, c, k, up):
            if k == 1:
                source = self.own.at[:, self.base + c]
            else:
                source = self.gz.at[c, (ring - k + 1 if up else k - 1) - 1]
            target = self.gz.at[c, (ring - k if up else k) - 1]
            if k == half:
                nodes = pl.ds(0 if up else NODE_DEV // 2, NODE_DEV // 2)
                source, target = source.at[nodes], target.at[nodes]
            way = 0 if up else 1
            return send(
                source, target, self.zsend.at[c, way, k - 1], self.zrecv.at[c, way, k - 1],
                above if up else below,
            )

        def across_x(self, c, k, plus):
            start, size = (slots.plus_group if plus else slots.minus_group)[k]
            base = slots.plus if plus else slots.minus
            way = 0 if plus else 1
            return send(
                (self.sp if plus else self.sm).at[c, pl.ds(start, size)],
                self.arr.at[c, pl.ds(base + start, size)],
                self.xsend.at[c, way, k], self.xrecv.at[c, way, k],
                right if plus else left,
            )

        def forward(self, c, k, plus):
            if plus:
                source = slots.plus + slots.plus_transit[k]
                target = slots.plus + slots.sent + k
                index = k
            else:
                source = slots.minus + slots.minus_transit[half if k == half else ring - k]
                target = slots.minus + slots.sent + k - 1
                index = k - 1
            way = 0 if plus else 1
            return send(
                self.arr.at[c, source], self.arr.at[c, target],
                self.fsend.at[c, way, index], self.frecv.at[c, way, index],
                right if plus else left,
            )

        def pick(self, c, dz, target):
            node = plan[target * devices + at(x, z + dz)]
            if dz == 0:
                return self.own[node, self.base + c]
            picked = self.gz[c, dz - 1, 0]
            for other in range(1, NODE_DEV):
                picked = jnp.where(node == other, self.gz[c, dz - 1, other], picked)
            return picked

        def group(self, c, k):
            dzs = [0] if k == 0 else [half] if k == half else [k, ring - k]
            for dz in dzs:
                self.sp[c, slots.plus_direct[dz]] = self.pick(c, dz, right)
                self.sm[c, slots.minus_direct[dz]] = self.pick(c, dz, left)
                if dz in slots.plus_transit:
                    self.sp[c, slots.plus_transit[dz]] = self.pick(c, dz, across)
                else:
                    self.sm[c, slots.minus_transit[dz]] = self.pick(c, dz, across)
            self.across_x(c, k, True).start()
            self.across_x(c, k, False).start()
            for dz in dzs:
                self.arr[c, dz] = self.pick(c, dz, me)

        def stage(self, c, k):
            for up in (True, False):
                if k >= 1:
                    self.hop(c, k, up).wait_recv()
                if k < half:
                    self.hop(c, k + 1, up).start()
            self.group(c, k)

        def relay(self, c, k):
            for plus in (True, False):
                self.across_x(c, k, plus).wait_recv()
                if k in (range(half) if plus else range(1, half + 1)):
                    self.forward(c, k, plus).start()

        def arrive(self, c):
            for k in range(half + 1):
                for plus in (True, False):
                    if k in (range(half) if plus else range(1, half + 1)):
                        self.forward(c, k, plus).wait_recv()

        def finish(self, c):
            for k in range(1, half + 1):
                for up in (True, False):
                    self.hop(c, k, up).wait_send()
            for k in range(half + 1):
                for plus in (True, False):
                    self.across_x(c, k, plus).wait_send()
                    if k in (range(half) if plus else range(1, half + 1)):
                        self.forward(c, k, plus).wait_send()

    per_group = heads // GROUPS
    main = [Stream(ssm, i * per_group, take(10)) for i in range(GROUPS)]
    side = Stream(convp, 0, take(10))

    def on_head(tick, offset, act):
        c = tick - offset
        for i in range(GROUPS):

            @pl.when((c >= i * per_group) & (c < (i + 1) * per_group))
            def _():
                act(main[i], c - i * per_group)

    def weigh(weights, values):
        high = weights.astype(jnp.bfloat16)
        low = (weights - high.astype(jnp.float32)).astype(jnp.bfloat16)
        return dot(high, values, ((1,), (0,))) + dot(low, values, ((1,), (0,)))

    def attend(message, keys, values, length):
        scale = HEAD**-0.5
        old = dot(message, keys, ((1,), (1,))) * scale
        spot = lax.broadcasted_iota(jnp.int32, old.shape, 1)
        old = jnp.where(spot < length, old, -jnp.inf)
        moved = dot(shift[...], message, ((1,), (0,))).astype(jnp.bfloat16)
        new = dot(message, moved, ((1,), (1,))) * scale + bias[...]
        top = jnp.maximum(jnp.max(old, 1, keepdims=True), jnp.max(new, 1, keepdims=True))
        old, new = jnp.exp(old - top), jnp.exp(new - top)
        total = jnp.sum(old, 1, keepdims=True) + jnp.sum(new, 1, keepdims=True)
        return (weigh(old, values) + weigh(new, message)) / total

    def pack(first, second):
        both = jnp.concatenate([comb[first], comb[second]], 0)
        return dot(gather[...], both, ((1,), (0,))).astype(jnp.bfloat16)

    def ask(d):
        return send(q_out.at[d], q_in.at[me], qsend.at[d], qrecv.at[me], d)

    def asked(d):
        return send(q_out.at[d], q_in.at[d], qsend.at[d], qrecv.at[d], d)

    def reply(d):
        return send(o_out.at[d], o_in.at[me], rsend.at[d], rrecv.at[me], d)

    def replied(d):
        return send(o_out.at[d], o_in.at[d], rsend.at[d], rrecv.at[d], d)

    def prepare():
        r = lax.broadcasted_iota(jnp.int32, (PAIR, PAIR), 0)
        c = lax.broadcasted_iota(jnp.int32, (PAIR, PAIR), 1)
        query = r + jnp.where(r >= 20, 12, 0)
        key = r - 20 + jnp.where(r >= 44, 28, 0)
        value = r - 24 + jnp.where(r >= 52, 28, 0)
        column = jnp.where(r < 40, query, jnp.where(r < 48, key, jnp.where(r < 56, value, -1)))
        gather[...] = jnp.where(column == c, 1.0, 0.0).astype(jnp.bfloat16)
        shift[...] = jnp.where((r >= 48) & (r < 56) & (c == r - 8), 1.0, 0.0).astype(jnp.bfloat16)
        same = jnp.where(c >= 52, 1, 0) == jnp.where(r >= 20, 1, 0)
        seen = (r < 40) & (c >= 48) & (c < 56) & same & ((c & 3) <= (r & 3))
        bias[...] = jnp.where(seen, 0.0, -jnp.inf)

        @pl.loop(0, rows)
        def _(row):
            query = q_v[row].astype(jnp.float32)
            lines = [query[:, g * HEAD : (g + 1) * HEAD] for g in range(GROUP)]
            fresh = nkv_v[row].astype(jnp.float32)
            lines += [fresh[0], fresh[1], jnp.zeros((4, HEAD), jnp.float32)]
            comb[row] = jnp.concatenate(lines, 0).astype(jnp.bfloat16)

    def ask_all():
        @pl.loop(0, devices)
        def _(step):
            d = (me + step) % devices
            message = pack(res_rows + plan[first_at + d], res_rows + plan[second_at + d])

            @pl.when(step == 0)
            def _():
                q_in[me] = message

            @pl.when(step != 0)
            def _():
                q_out[d] = message
                ask(d).start()

    def serve(step):
        d = (me + devices - step) % devices

        @pl.when(step != 0)
        def _():
            asked(d).wait_recv()

        node = plan[d * devices + me]
        result = attend(q_in[d], kv_nodes[node, 0], kv_nodes[node, 1], len_nodes[me * NODE_DEV + node])
        result = result[:BACK].astype(jnp.bfloat16)

        @pl.when(step == 0)
        def _():
            o_in[me] = result

        @pl.when(step != 0)
        def _():
            o_out[d] = result
            reply(d).start()

    def put_attended(row, value):
        value = jnp.where(alive[row] > 0, value, 0.0).astype(jnp.bfloat16)
        for g in range(GROUP):
            att[row, :, g * HEAD : (g + 1) * HEAD] = value[4 * g : 4 * g + 4]

    def resident(row):
        put_attended(row, attend(pack(row, row), kv_res[row, 0], kv_res[row, 1], len_res[row])[:20])

    def convolve():
        for j in range(KERNEL - 1):
            ux[j, 0:res_rows] = cr_v[j].astype(jnp.float32)
            ub[j, 0:res_rows] = cbr_v[j].astype(jnp.float32)
        carr = side.arr
        for child in range(child_dev):
            lines = carr[0, plan[place_at + child]].astype(jnp.float32)
            at_row = slice(res_rows + child, res_rows + child + 1)
            line = 0
            for target in (ux, ub):
                for j in range(KERNEL - 1):
                    for begin in range(0, target.shape[2], STATE):
                        target[j, at_row, begin : begin + STATE] = lines[line : line + 1]
                        line += 1
        fresh_x = x_v[...].astype(jnp.float32)
        fresh_b = bc_v[...].astype(jnp.float32)
        for t in range(STEPS):
            ux[KERNEL - 1 + t] = fresh_x[:, t, :]
            ub[KERNEL - 1 + t] = fresh_b[:, t, :]
        weights_x = wx_v[...].astype(jnp.float32)
        weights_b = wbc_v[...].astype(jnp.float32)

        def mix(source, weights, t):
            total = weights[0:1] * source[t]
            for tap in range(1, KERNEL):
                total = total + weights[tap : tap + 1] * source[t + tap]
            return silu(total)

        lane = lax.broadcasted_iota(jnp.int32, (1, features), 1)

        def spread(table):
            value = jnp.zeros((1, features), jnp.float32)
            for h in range(heads):
                inside = (lane >= h * SSM_HEAD) & (lane < (h + 1) * SSM_HEAD)
                value = jnp.where(inside, table[h], value)
            return value

        rate, offset, skip = -jnp.exp(spread(a_log)), spread(dt_bias), spread(skip_gain)
        head = lax.broadcasted_iota(jnp.int32, (heads, features), 0) * SSM_HEAD
        lanes = lax.broadcasted_iota(jnp.int32, (heads, features), 1)
        one_hot = jnp.where((lanes >= head) & (lanes < head + SSM_HEAD), 1.0, 0.0).astype(jnp.bfloat16)
        b_list = []
        c_parts[...] = jnp.zeros(c_parts.shape, jnp.float32)
        b_parts[...] = jnp.zeros(b_parts.shape, jnp.float32)
        w_parts[...] = jnp.zeros(w_parts.shape, jnp.float32)
        since = []
        for t in range(STEPS):
            both = mix(ub, weights_b, t)
            b, c = both[:, :STATE], both[:, STATE:]
            b_list.append(b)
            for part, piece in enumerate(split(c, 3)):
                c_parts[part * 4 + t] = piece
            high, low = split(b, 2)
            b_parts[t], b_parts[4 + t], b_parts[8 + t] = high, low, high
            dt = softplus(dot(dt_v[t], one_hot, ((0,), (0,))) + offset)
            decay = jnp.exp(rate * dt)
            mixed = mix(ux, weights_x, t)
            carried[t] = decay if t == 0 else carried[t - 1] * decay
            since = [value * decay for value in since] + [dt * mixed]
            total = skip * mixed
            for s in range(t + 1):
                total = total + since[s] * jnp.sum(c * b_list[s], 1, keepdims=True)
            rest[t] = total
        for s in range(STEPS):
            high, low = split(since[s], 2)
            w_parts[s], w_parts[4 + s], w_parts[8 + s] = high, high, low

    def new_copy(row, i):
        span = pl.ds(i * per_group, per_group)
        return pltpu.make_async_copy(new_v.at[row, span], new_out.at[row, span], new_sem.at[row, i])

    def update(row, i, state):
        span = slice(i * per_group * SSM_HEAD, (i + 1) * per_group * SSM_HEAD)
        width = per_group * SSM_HEAD
        here = pl.ds(row, 1)
        state = state.reshape(width, STATE)
        c_row = c_parts[:, here, :].reshape(16, STATE).astype(jnp.bfloat16)
        b_row = b_parts[:, here, :].reshape(16, STATE).astype(jnp.bfloat16)
        w_row = w_parts[:, here, span].reshape(16, width).astype(jnp.bfloat16)
        got = dot(c_row, state, ((1,), (1,)))
        read[:, here, span] = (got[0:4] + got[4:8] + got[8:12]).reshape(STEPS, 1, width)
        added = dot(w_row, b_row, ((0,), (0,)))
        last = carried[STEPS - 1, here, span]
        for h in range(per_group):
            part = slice(h * SSM_HEAD, (h + 1) * SSM_HEAD)
            factor = last[:, h * SSM_HEAD : h * SSM_HEAD + 1]
            new = factor * state[part].astype(jnp.float32) + added[part]
            new_v[row, i * per_group + h] = new.astype(jnp.bfloat16)
        new_copy(row, i).start()

    def update_resident(row):
        for i in range(GROUPS):
            update(row, i, res[row, i * per_group : (i + 1) * per_group])

    def update_child(child, i):
        update(res_rows + child, i, main[i].arr[:, plan[place_at + child]])

    batch = 4
    begin = [2 * k for k in range(half + 1)]
    ticks = heads + begin[half] + 1
    ready = begin[half] + 2
    landed_at = per_group + begin[half] + 1
    share = -(-child_dev // (ticks - landed_at))

    @pl.loop(0, ticks)
    def _(tick):
        for k in range(half, -1, -1):

            @pl.when(tick == begin[k])
            def _():
                side.stage(0, k)

            on_head(tick, begin[k], lambda stream, c: stream.stage(c, k))
        for k in range(half, -1, -1):

            @pl.when(tick == begin[k] + 1)
            def _():
                side.relay(0, k)

            on_head(tick, begin[k] + 1, lambda stream, c: stream.relay(c, k))

        @pl.when(tick == 0)
        def _():
            prepare()
            ask_all()

        @pl.when(tick == 1)
        def _():
            @pl.loop(0, res_rows)
            def _(row):
                resident(row)

        @pl.when((tick >= 2) & (tick < 2 + devices // batch))
        def _():
            @pl.loop(0, batch)
            def _(i):
                serve((tick - 2) * batch + i)

        @pl.when(tick == ready)
        def _():
            side.arrive(0)
            convolve()

            @pl.loop(0, res_rows)
            def _(row):
                update_resident(row)

        if GROUPS > 1:

            @pl.when(tick == landed_at)
            def _():
                @pl.loop(0, per_group)
                def _(c):
                    main[0].arrive(c)

            @pl.when(tick >= landed_at)
            def _():
                @pl.loop(0, share)
                def _(i):
                    child = (tick - landed_at) * share + i

                    @pl.when(child < child_dev)
                    def _():
                        update_child(child, 0)

    @pl.loop(1, devices)
    def _(step):
        d = (me + step) % devices
        replied(d).wait_recv()

    @pl.loop(0, child_dev)
    def _(child):
        value = o_in[plan[src_at + child]].astype(jnp.float32)
        put_attended(res_rows + child, jnp.where(plan[which_at + child] == 1, value[20:40], value[0:20]))

    @pl.loop(0, per_group)
    def _(c):
        main[-1].arrive(c)

    @pl.loop(0, child_dev)
    def _(child):
        update_child(child, GROUPS - 1)

    gated = []
    gates = g_v[...].astype(jnp.float32)
    lane = lax.broadcasted_iota(jnp.int32, (rows, 128), 1)
    total = jnp.zeros((rows, 128), jnp.float32)
    for t in range(STEPS):
        value = (carried[t] * read[t] + rest[t]) * silu(gates[:, t, :])
        gated.append(value)
        total = jnp.where(lane == t, jnp.sum(value * value, 1, keepdims=True), total)
    sums[...] = total

    def share_sums(d, slot):
        return pltpu.make_async_remote_copy(
            src_ref=sums, dst_ref=landed.at[slot], send_sem=psend.at[d], recv_sem=precv.at[slot],
            device_id=(me, d), device_id_type=MESH,
        )

    if peers > 1:

        @pl.loop(1, peers)
        def _(step):
            share_sums((tensor + step) % peers, tensor).start()

    for stream, count in [(side, 1)] + [(m, per_group) for m in main]:

        @pl.loop(0, count)
        def _(c):
            stream.finish(c)

    @pl.loop(1, devices)
    def _(step):
        d = (me + step) % devices
        ask(d).wait_send()
        reply(d).wait_send()

    if peers > 1:

        @pl.loop(1, peers)
        def _(step):
            d = (tensor + step) % peers
            share_sums(d, d).wait_recv()

        landed[tensor] = sums[...]
        total = landed[0]
        for d in range(1, peers):
            total = total + landed[d]
    scale = lax.rsqrt(total / INNER + EPSILON)
    row_of = lax.broadcasted_iota(jnp.int32, (rows, 128), 0)
    living = jnp.zeros((rows, 128), jnp.int32)
    for row in range(rows):
        living = jnp.where(row_of == row, alive[row], living)
    for t in range(STEPS):
        result = gated[t] * scale[:, t : t + 1] * gain_v[...]
        ssm_out[t] = jnp.where(living[:, 0:1] > 0, result, 0.0).astype(jnp.bfloat16)

    @pl.loop(0, rows)
    def _(row):
        for i in range(GROUPS):
            new_copy(row, i).wait()

    if peers > 1:

        @pl.loop(1, peers)
        def _(step):
            share_sums((tensor + step) % peers, tensor).wait_send()


def run_round(plan, scalars, arrays, ring, peers):
    slots = Slots(ring)
    half = ring // 2
    devices = COLUMNS * ring
    ssm, res, queries, gate = arrays[0], arrays[1], arrays[4], arrays[7]
    heads = ssm.shape[1]
    rows, res_rows = queries.shape[0], res.shape[0]
    child_dev = rows - res_rows
    features = heads * SSM_HEAD
    per_group = heads // GROUPS
    bf16, f32 = jnp.bfloat16, jnp.float32
    dma = pltpu.SemaphoreType.DMA

    def stream(count, height):
        return [
            pltpu.VMEM((count, ring - 1, NODE_DEV, height, STATE), bf16),
            pltpu.VMEM((count, slots.sent, height, STATE), bf16),
            pltpu.VMEM((count, slots.sent, height, STATE), bf16),
            pltpu.VMEM((count, slots.total, height, STATE), bf16),
            dma((count, 2, half)), dma((count, 2, half)),
            dma((count, 2, half + 1)), dma((count, 2, half + 1)),
            dma((count, 2, half)), dma((count, 2, half)),
        ]

    scratch = [pltpu.VMEM(a.shape, a.dtype) for a in arrays] + [dma((len(arrays),))]
    scratch += [
        pltpu.VMEM((rows, BLOCK, HEAD), bf16),
        pltpu.VMEM((NODE_DEV, 1, 16, STATE), bf16),
        pltpu.VMEM((rows, heads, SSM_HEAD, STATE), bf16),
        pltpu.VMEM((PAIR, PAIR), bf16),
        pltpu.VMEM((PAIR, PAIR), bf16),
        pltpu.VMEM((PAIR, PAIR), f32),
    ]
    taps = KERNEL - 1 + STEPS
    scratch += [
        pltpu.VMEM((taps, rows, features), f32),
        pltpu.VMEM((taps, rows, 2 * STATE), f32),
        pltpu.VMEM((16, rows, STATE), f32),
        pltpu.VMEM((16, rows, STATE), f32),
        pltpu.VMEM((16, rows, features), f32),
        pltpu.VMEM((STEPS, rows, features), f32),
        pltpu.VMEM((STEPS, rows, features), f32),
        pltpu.VMEM((STEPS, rows, features), f32),
    ]
    scratch += [
        pltpu.VMEM((devices, PAIR, HEAD), bf16),
        pltpu.VMEM((devices, PAIR, HEAD), bf16),
        pltpu.VMEM((devices, BACK, HEAD), bf16),
        pltpu.VMEM((devices, BACK, HEAD), bf16),
    ] + [dma((devices,))] * 4
    scratch += [
        pltpu.VMEM((rows, 128), f32),
        pltpu.VMEM((peers, rows, 128), f32),
        dma((peers,)),
        dma((peers,)),
        dma((rows, GROUPS)),
    ]
    for _ in range(GROUPS):
        scratch += stream(per_group, SSM_HEAD)
    scratch += stream(1, 16)
    smem = pl.BlockSpec(memory_space=pltpu.SMEM)
    vmem = pl.BlockSpec(memory_space=pltpu.VMEM)
    anywhere = pl.BlockSpec(memory_space=pl.ANY)
    return pl.pallas_call(
        functools.partial(round_kernel, slots, heads, res_rows, child_dev, peers),
        out_shape=[
            jax.ShapeDtypeStruct(queries.shape, bf16),
            jax.ShapeDtypeStruct((STEPS, rows, features), bf16),
            jax.ShapeDtypeStruct((rows,) + ssm.shape[1:], bf16),
        ],
        in_specs=[smem] * (1 + len(scalars)) + [anywhere] * len(arrays),
        out_specs=[vmem, vmem, anywhere],
        scratch_shapes=scratch,
        compiler_params=pltpu.CompilerParams(
            collective_id=0, has_side_effects=True, vmem_limit_bytes=60 * 1024 * 1024
        ),
        name="round",
    )(plan, *scalars, *arrays)


def per_device(
    ssm_resident, ssm_nodes, conv_resident, conv_nodes, convbc_resident, convbc_nodes,
    kv_resident, kv_nodes, len_resident, len_nodes, parents, alive_flags, queries, new_kv,
    x_in, gate_in, bc_in, dt_in, conv_x_weight, conv_bc_weight, a_log, dt_bias, skip_gain, norm_gain,
):
    devices = lax.axis_size("dp")
    me = lax.axis_index("dp")
    ring = devices // COLUMNS
    child_dev = parents.shape[0] // devices

    grouped = parents.reshape(devices, child_dev)
    match = (grouped // NODE_DEV)[:, None, :] == jnp.arange(devices)[None, :, None]
    tab = jnp.max(jnp.where(match, (grouped % NODE_DEV)[:, None, :], 0), axis=2).reshape(-1)
    own = lax.dynamic_slice_in_dim(parents, me * child_dev, child_dev)
    child_src = own // NODE_DEV
    mine = child_src[None, :] == jnp.arange(devices)[:, None]
    number = jnp.arange(child_dev)[None, :]
    first = jnp.min(jnp.where(mine, number, child_dev - 1), axis=1)
    second = jnp.max(jnp.where(mine, number, 0), axis=1)
    child_which = jnp.sum(jnp.where(mine & (number > first[:, None]), 1, 0), axis=0)
    relative = (
        (child_src // ring - me // ring) % COLUMNS * ring + (child_src % ring - me % ring) % ring
    )
    spot = jnp.arange(devices)[None, :] == relative[:, None]
    place = jnp.sum(jnp.where(spot, jnp.asarray(Slots(ring).table())[None, :], 0), axis=1)
    plan = jnp.concatenate([tab, first, second, child_src, child_which, place]).astype(jnp.int32)
    turned = [jnp.transpose(a, (1, 0, 2)) for a in (conv_resident, convbc_resident, conv_nodes, convbc_nodes)]
    arrays = [
        ssm_nodes, ssm_resident, kv_nodes, kv_resident, queries, new_kv, x_in, gate_in, bc_in,
        jnp.transpose(dt_in, (1, 2, 0)), *turned, conv_x_weight, conv_bc_weight, norm_gain[None, :],
    ]
    scalars = [len_nodes, len_resident, alive_flags, a_log, dt_bias, skip_gain]
    attn, ssm_out, new_ssm = run_round(plan, scalars, arrays, ring, lax.axis_size("tensor"))
    return attn, jnp.transpose(ssm_out, (1, 0, 2)), new_ssm


def solution(mesh):
    return jax.shard_map(
        per_device,
        mesh=mesh,
        in_specs=(
            P("dp", "tensor", None, None),
            P("dp", "tensor", None, None),
            P("dp", None, "tensor"),
            P("dp", None, "tensor"),
            P("dp", None, None),
            P("dp", None, None),
            P("dp", None, None, "tensor"),
            P("dp", None, None, "tensor"),
            P("dp"),
            P(),
            P(),
            P("dp"),
            P("dp", None, "tensor"),
            P("dp", None, None, "tensor"),
            P("dp", None, "tensor"),
            P("dp", None, "tensor"),
            P("dp", None, None),
            P("dp", None, "tensor"),
            P(None, "tensor"),
            P(),
            P("tensor"),
            P("tensor"),
            P("tensor"),
            P("tensor"),
        ),
        out_specs=(P("dp", None, "tensor"), P("dp", None, "tensor"), P("dp", "tensor", None, None)),
        check_vma=False,
    )
```

time: 203 us -> 159 us (0.78)
  Pallas kernels: 164 us -> 145 us
  local copies, waits for them, and re-layouts: 28.2 us -> 11.3 us
  other arithmetic: 8.03 us -> 2.11 us
    pallas_call x3 -> x1, Pallas kernels: 164 us -> 145 us  [run_round(): pl.pallas_call(functools.partial(round_kernel, slots, heads, res_rows, ch...]
    reshape x20 -> x0, local copies, waits for them, and re-layouts: 6.13 us -> none  [the longest x1 1.66 us: per_device(): read.reshape(lines, features)]
    unnamed x52 -> x3, local copies, waits for them, and re-layouts: 14.8 us -> 9.79 us
    concatenate x4 -> x0, other arithmetic: 2.93 us -> none  [the longest x2 1.95 us: padded(): return jnp.concatenate(pieces + [jnp.zeros_like(pieces[0])], 1)]
where the time goes in v2:
time: 159 us
  Pallas kernels  145 us (91%)
  local copies, waits for them, and re-layouts  11.3 us (7%)
  other arithmetic  2.11 us (1%)
    pallas_call x1, Pallas kernels, run_round(): pl.pallas_call(functools.partial(round_kernel, slots, heads, res_rows, ch...  145 us
    unnamed x3, local copies, waits for them, and re-layouts  9.79 us

profile of v2, /device:TPU:1, one launch (start us, length us, event | category | flops | bytes accessed | tf_op | source)
XLA Modules:
  0.0 158.6 jit_solution(685499952232680553)
XLA Ops:
  0.7 0.8 fusion.3
  1.4 0.8 select_reduce_fusion.4
  2.3 0.1 select_reduce_fusion.3
  2.4 0.1 select_reduce_fusion.1
  2.5 0.8 reshape.65
  3.3 0.2 select_reduce_fusion
  3.5 0.1 reshape.66
  3.6 0.7 concatenate.3.plan
  4.3 144.5 %round.1 = (bf16[24,4,640]{2,1,0:T(4,128)(2,1)}, bf16[4,24,512]{2,1,0:T(8,128)(2,1)}, bf16[24,8,64,256]{3,2,1,0:T(8,128)(2,1)}) custom-call(s32[1136]{0:T(1024)} %concatenate.3.plan, s32[128]{0:T(128)} %len_nodes.1, s32[8]{0:T(128)} %len_res.1, s32[24]{0:T(128)} %alive.1, f32[8]{0:T(128)} %a_log.1, f32[8]{0:T(128)} %dt_bias.1, f32[8]{0:T(128)} %skip_gain.1, ...), custom_call_target="tpu_custom_call" | custom-call | tf_op jit(solution)/shard_map/round/pallas_call | solution.py:701
  148.8 1.6 copy.30
  150.4 1.6 %copy.33 = bf16[24,4,640]{2,1,0:T(4,128)(2,1)} copy(bf16[24,4,640]{2,1,0:T(4,128)(2,1)} %get-tuple-element.27) | data formatting | bytes 245760
  152.0 6.6 %copy.34 = bf16[24,8,64,256]{3,2,1,0:T(8,128)(2,1)} copy(bf16[24,8,64,256]{3,2,1,0:T(8,128)(2,1)} %get-tuple-element.29) | data formatting | bytes 12582912
  (1 shorter events, 0.0 us)

commit v3 on v2

--- a/solution.py
+++ b/solution.py
@@ -62,7 +62,13 @@
 PAIR = 64
 BACK = 48
 BLOCK = 32
-GROUPS = 2
+RING_GROUPS = 2
+ROUTE_HEADS = (2, 2, 2, 2)
+
+SLOTS, X_SLOTS, X_START, LAG = 12, 11, 7, 3
+REPLY = 0
+STRIDE = 12
+PLACE_ROW = 2 * (SLOTS + X_SLOTS)
 
 
 def dot(a, b, dims):
@@ -87,8 +93,8 @@
 
 
 def round_kernel(
-    slots, heads, res_rows, child_dev, peers,
-    plan, len_nodes, len_res, alive, a_log, dt_bias, skip_gain,
+    slots, heads, res_rows, child_dev, peers, routed,
+    plan, routes, len_nodes, len_res, alive, a_log, dt_bias, skip_gain,
     ssm_h, res_h, kvn_h, kvr_h, q_h, nkv_h, x_h, g_h, bc_h, dt_h, cr_h, cbr_h, cn_h, cbn_h, wx_h, wbc_h, gain_h,
     att, ssm_out, new_out,
     *scratch,
@@ -110,6 +116,7 @@
     (new_sem,) = take(1)
 
     ring, half = slots.ring, slots.half
+    groups = len(ROUTE_HEADS) if routed else RING_GROUPS
     devices = COLUMNS * ring
     rows = res_rows + child_dev
     features = heads * SSM_HEAD
@@ -178,7 +185,7 @@
 
     class Stream:
         def __init__(self, own, base, refs):
-            self.own, self.base = own, base
+            self.own, self.base, self.count = own, base, refs[0].shape[0]
             (self.gz, self.sp, self.sm, self.arr,
              self.zsend, self.zrecv, self.xsend, self.xrecv, self.fsend, self.frecv) = refs
 
@@ -277,13 +284,115 @@
                     if k in (range(half) if plus else range(1, half + 1)):
                         self.forward(c, k, plus).wait_send()
 
-    per_group = heads // GROUPS
-    main = [Stream(ssm, i * per_group, take(10)) for i in range(GROUPS)]
-    side = Stream(convp, 0, take(10))
+    class Route:
+        def __init__(self, own, base, count, refs):
+            self.own, self.base, self.count = own, base, count
+            self.inn, self.out, self.zsend, self.zrecv, self.xsend, self.xrecv = refs
+
+        def copy(self, way, slot):
+            start = (0, SLOTS, 2 * SLOTS, 2 * SLOTS + X_SLOTS)[way]
+            if way < 2:
+                sems = self.zsend.at[way, slot], self.zrecv.at[way, slot]
+            else:
+                sems = self.xsend.at[way - 2, slot], self.xrecv.at[way - 2, slot]
+            return send(
+                self.out.at[start + slot], self.inn.at[start + slot], *sems,
+                (above, below, right, left)[way],
+            )
+
+        def first(self, code):
+            node = jnp.minimum(code, NODE_DEV - 1)
+            return tuple(self.own[node, self.base + h] for h in range(self.count))
+
+        def choose(self, code, slot, held):
+            return tuple(
+                jnp.where(code == NODE_DEV + slot, self.inn[slot, h], held[h]) for h in range(self.count)
+            )
+
+        def put(self, way, slot, value):
+            start = (0, SLOTS, 2 * SLOTS, 2 * SLOTS + X_SLOTS)[way]
+            for h in range(self.count):
+                self.out[start + slot, h] = value[h]
+            self.copy(way, slot).start()
+
+        def z_step(self, step):
+            landed = step - LAG
+
+            @pl.when((landed >= 0) & (landed < SLOTS))
+            def _():
+                for way in (0, 1):
+                    self.copy(way, landed).wait_recv()
+
+            @pl.when((step >= 0) & (step < SLOTS))
+            def _():
+                for way in (0, 1):
+                    code = routes[way * SLOTS + step, me]
+                    value = lax.fori_loop(
+                        0, jnp.maximum(step - LAG + 1, 0),
+                        lambda r, held: self.choose(code, way * SLOTS + r, held), self.first(code),
+                    )
+                    self.put(way, step, value)
+
+        def x_step(self, step):
+            slot = step - X_START
+            landed = slot - LAG
+
+            @pl.when((landed >= 0) & (landed < X_SLOTS))
+            def _():
+                for way in (2, 3):
+                    self.copy(way, landed).wait_recv()
+
+            @pl.when((slot >= 0) & (slot < X_SLOTS))
+            def _():
+                codes = [routes[2 * SLOTS + i * X_SLOTS + slot, me] for i in range(2)]
+
+                def from_z(r, held):
+                    result = []
+                    for code, value in zip(codes, held):
+                        for start in (0, SLOTS):
+                            value = self.choose(code, start + r, value)
+                        result.append(value)
+                    return tuple(result)
+
+                def from_x(r, held):
+                    return tuple(
+                        self.choose(codes[i], 2 * SLOTS + i * X_SLOTS + r, held[i]) for i in range(2)
+                    )
+
+                held = tuple(self.first(code) for code in codes)
+                held = lax.fori_loop(0, jnp.minimum(step - LAG + 1, SLOTS), from_z, held)
+                held = lax.fori_loop(0, jnp.maximum(landed + 1, 0), from_x, held)
+                for i in range(2):
+                    self.put(2 + i, slot, held[i])
+
+        def arrived(self, child):
+            code = routes[PLACE_ROW + child, me]
+            slot = jnp.maximum(code - NODE_DEV, 0)
+            held = self.first(code)
+            return [jnp.where(code < NODE_DEV, held[h], self.inn[slot, h]) for h in range(self.count)]
+
+        def finish(self, _):
+            @pl.loop(0, SLOTS)
+            def _(slot):
+                for way in (0, 1):
+                    self.copy(way, slot).wait_send()
+
+            @pl.loop(0, X_SLOTS)
+            def _(slot):
+                for way in (2, 3):
+                    self.copy(way, slot).wait_send()
+
+    per_group = heads // groups
+    if routed:
+        main = [Route(ssm, sum(ROUTE_HEADS[:i]), ROUTE_HEADS[i], take(6)) for i in range(groups)]
+        side = Route(convp, 0, 1, take(6))
+    else:
+        main = [Stream(ssm, i * per_group, take(10)) for i in range(groups)]
+        side = Stream(convp, 0, take(10))
 
     def on_head(tick, offset, act):
         c = tick - offset
-        for i in range(GROUPS):
+        for i in range(groups):
 
             @pl.when((c >= i * per_group) & (c < (i + 1) * per_group))
             def _():
@@ -310,7 +419,7 @@
         both = jnp.concatenate([comb[first], comb[second]], 0)
         return dot(gather[...], both, ((1,), (0,))).astype(jnp.bfloat16)
 
-    def ask(d):
+    def asking(d):
         return send(q_out.at[d], q_in.at[me], qsend.at[d], qrecv.at[me], d)
 
     def asked(d):
@@ -343,11 +452,13 @@
             lines += [fresh[0], fresh[1], jnp.zeros((4, HEAD), jnp.float32)]
             comb[row] = jnp.concatenate(lines, 0).astype(jnp.bfloat16)
 
-    def ask_all():
-        @pl.loop(0, devices)
-        def _(step):
+    def ask(steps):
+        messages = []
+        for step in steps:
             d = (me + step) % devices
-            message = pack(res_rows + plan[first_at + d], res_rows + plan[second_at + d])
+            messages.append(pack(res_rows + plan[first_at + d], res_rows + plan[second_at + d]))
+        for step, message in zip(steps, messages):
+            d = (me + step) % devices
 
             @pl.when(step == 0)
             def _():
@@ -356,43 +467,57 @@
             @pl.when(step != 0)
             def _():
                 q_out[d] = message
-                ask(d).start()
-
-    def serve(step):
-        d = (me + devices - step) % devices
-
-        @pl.when(step != 0)
-        def _():
-            asked(d).wait_recv()
-
-        node = plan[d * devices + me]
-        result = attend(q_in[d], kv_nodes[node, 0], kv_nodes[node, 1], len_nodes[me * NODE_DEV + node])
-        result = result[:BACK].astype(jnp.bfloat16)
-
-        @pl.when(step == 0)
-        def _():
-            o_in[me] = result
-
-        @pl.when(step != 0)
-        def _():
-            o_out[d] = result
-            reply(d).start()
+                asking(d).start()
+
+    def serve(steps):
+        served = [(me + devices - step) % devices for step in steps]
+        for step, d in zip(steps, served):
+
+            @pl.when(step != 0)
+            def _():
+                asked(d).wait_recv()
+
+        results = []
+        for d in served:
+            node = plan[d * devices + me]
+            length = len_nodes[me * NODE_DEV + node]
+            result = attend(q_in[d], kv_nodes[node, 0], kv_nodes[node, 1], length)
+            results.append(result[:BACK].astype(jnp.bfloat16))
+        for step, d, result in zip(steps, served, results):
+
+            @pl.when(step == 0)
+            def _():
+                o_in[me] = result
+
+            @pl.when(step != 0)
+            def _():
+                o_out[d] = result
+                if not routed:
+                    reply(d).start()
 
     def put_attended(row, value):
         value = jnp.where(alive[row] > 0, value, 0.0).astype(jnp.bfloat16)
         for g in range(GROUP):
             att[row, :, g * HEAD : (g + 1) * HEAD] = value[4 * g : 4 * g + 4]
 
-    def resident(row):
-        put_attended(row, attend(pack(row, row), kv_res[row, 0], kv_res[row, 1], len_res[row])[:20])
+    def resident(lines):
+        messages = [pack(row, row) for row in lines]
+        results = [
+            attend(message, kv_res[row, 0], kv_res[row, 1], len_res[row])[:20]
+            for row, message in zip(lines, messages)
+        ]
+        for row, result in zip(lines, results):
+            put_attended(row, result)
 
     def convolve():
         for j in range(KERNEL - 1):
             ux[j, 0:res_rows] = cr_v[j].astype(jnp.float32)
             ub[j, 0:res_rows] = cbr_v[j].astype(jnp.float32)
-        carr = side.arr
         for child in range(child_dev):
-            lines = carr[0, plan[place_at + child]].astype(jnp.float32)
+            if routed:
+                lines = side.arrived(child)[0].astype(jnp.float32)
+            else:
+                lines = side.arr[0, plan[place_at + child]].astype(jnp.float32)
             at_row = slice(res_rows + child, res_rows + child + 1)
             line = 0
             for target in (ux, ub):
@@ -454,127 +579,186 @@
             w_parts[s], w_parts[4 + s], w_parts[8 + s] = high, high, low
 
     def new_copy(row, i):
-        span = pl.ds(i * per_group, per_group)
+        span = pl.ds(main[i].base, main[i].count)
         return pltpu.make_async_copy(new_v.at[row, span], new_out.at[row, span], new_sem.at[row, i])
 
     def update(row, i, state):
-        span = slice(i * per_group * SSM_HEAD, (i + 1) * per_group * SSM_HEAD)
-        width = per_group * SSM_HEAD
+        base, count = main[i].base, main[i].count
+        span = slice(base * SSM_HEAD, (base + count) * SSM_HEAD)
+        width = count * SSM_HEAD
         here = pl.ds(row, 1)
         state = state.reshape(width, STATE)
         c_row = c_parts[:, here, :].reshape(16, STATE).astype(jnp.bfloat16)
         b_row = b_parts[:, here, :].reshape(16, STATE).astype(jnp.bfloat16)
-        w_row = w_parts[:, here, span].reshape(16, width).astype(jnp.bfloat16)
+        window = span.start // STATE * STATE
+        w_row = w_parts[:, here, window : max(window + STATE, span.stop)]
+        w_row = w_row[:, :, span.start - window : span.stop - window].reshape(16, width).astype(jnp.bfloat16)
         got = dot(c_row, state, ((1,), (1,)))
-        read[:, here, span] = (got[0:4] + got[4:8] + got[8:12]).reshape(STEPS, 1, width)
+        got = got[0:4] + got[4:8] + got[8:12]
+        read[row, 0:STEPS, span] = got
         added = dot(w_row, b_row, ((0,), (0,)))
-        last = carried[STEPS - 1, here, span]
-        for h in range(per_group):
+        last = carried[STEPS - 1 : STEPS, here, window : max(window + STATE, span.stop)]
+        last = last.reshape(1, last.shape[2])[:, span.start - window : span.stop - window]
+        for h in range(count):
             part = slice(h * SSM_HEAD, (h + 1) * SSM_HEAD)
             factor = last[:, h * SSM_HEAD : h * SSM_HEAD + 1]
             new = factor * state[part].astype(jnp.float32) + added[part]
-            new_v[row, i * per_group + h] = new.astype(jnp.bfloat16)
-        new_copy(row, i).start()
-
-    def update_resident(row):
-        for i in range(GROUPS):
-            update(row, i, res[row, i * per_group : (i + 1) * per_group])
-
-    def update_child(child, i):
-        update(res_rows + child, i, main[i].arr[:, plan[place_at + child]])
-
-    batch = 4
-    begin = [2 * k for k in range(half + 1)]
-    ticks = heads + begin[half] + 1
-    ready = begin[half] + 2
-    landed_at = per_group + begin[half] + 1
-    share = -(-child_dev // (ticks - landed_at))
-
-    @pl.loop(0, ticks)
-    def _(tick):
-        for k in range(half, -1, -1):
-
-            @pl.when(tick == begin[k])
-            def _():
-                side.stage(0, k)
-
-            on_head(tick, begin[k], lambda stream, c: stream.stage(c, k))
-        for k in range(half, -1, -1):
-
-            @pl.when(tick == begin[k] + 1)
-            def _():
-                side.relay(0, k)
-
-            on_head(tick, begin[k] + 1, lambda stream, c: stream.relay(c, k))
-
-        @pl.when(tick == 0)
+            new_v[row, base + h] = new.astype(jnp.bfloat16)
+    def update_resident(lines):
+        for row in lines:
+            for i in range(groups):
+                update(row, i, res[row, main[i].base : main[i].base + main[i].count])
+        for row in lines:
+            for i in range(groups):
+                new_copy(row, i).start()
+
+    def update_child(children, i):
+        for child in children:
+            if routed:
+                state = jnp.stack(main[i].arrived(child))
+            else:
+                state = main[i].arr[:, plan[place_at + child]]
+            update(res_rows + child, i, state)
+        for child in children:
+            new_copy(res_rows + child, i).start()
+
+    def spread_over(tick, start, per_tick, total, act):
+        steps = -(-total // per_tick)
+
+        @pl.when((tick >= start) & (tick < start + steps))
         def _():
-            prepare()
-            ask_all()
-
-        @pl.when(tick == 1)
-        def _():
-            @pl.loop(0, res_rows)
-            def _(row):
-                resident(row)
-
-        @pl.when((tick >= 2) & (tick < 2 + devices // batch))
-        def _():
-            @pl.loop(0, batch)
-            def _(i):
-                serve((tick - 2) * batch + i)
-
-        @pl.when(tick == ready)
-        def _():
-            side.arrive(0)
-            convolve()
-
-            @pl.loop(0, res_rows)
-            def _(row):
-                update_resident(row)
-
-        if GROUPS > 1:
-
-            @pl.when(tick == landed_at)
-            def _():
-                @pl.loop(0, per_group)
-                def _(c):
-                    main[0].arrive(c)
-
-            @pl.when(tick >= landed_at)
-            def _():
-                @pl.loop(0, share)
+            act([(tick - start) * per_tick + j for j in range(per_tick)])
+
+    def reply_all():
+        @pl.loop(1, devices)
+        def _(step):
+            reply((me + devices - step) % devices).start()
+
+    def gather_replies():
+        @pl.loop(1, devices)
+        def _(step):
+            replied((me + step) % devices).wait_recv()
+
+        @pl.loop(0, child_dev)
+        def _(child):
+            value = o_in[plan[src_at + child]].astype(jnp.float32)
+            put_attended(res_rows + child, jnp.where(plan[which_at + child] == 1, value[20:40], value[0:20]))
+
+    def run_ring():
+        batch = 4
+        begin = [2 * k for k in range(half + 1)]
+        ticks = heads + begin[half] + 1
+        ready = begin[half] + 2
+        landed_at = per_group + begin[half] + 1
+        share = -(-child_dev // (ticks - landed_at))
+
+        @pl.loop(0, ticks)
+        def _(tick):
+            for k in range(half, -1, -1):
+
+                @pl.when(tick == begin[k])
+                def _():
+                    side.stage(0, k)
+
+                on_head(tick, begin[k], lambda stream, c: stream.stage(c, k))
+            for k in range(half, -1, -1):
+
+                @pl.when(tick == begin[k] + 1)
+                def _():
+                    side.relay(0, k)
+
+                on_head(tick, begin[k] + 1, lambda stream, c: stream.relay(c, k))
+
+            @pl.when(tick == 0)
+            def _():
+                prepare()
+                pl.loop(0, devices)(lambda step: ask([step]))
+
+            @pl.when(tick == 1)
+            def _():
+                @pl.loop(0, res_rows)
+                def _(row):
+                    resident([row])
+
+            @pl.when((tick >= 2) & (tick < 2 + devices // batch))
+            def _():
+                @pl.loop(0, batch)
                 def _(i):
-                    child = (tick - landed_at) * share + i
-
-                    @pl.when(child < child_dev)
-                    def _():
-                        update_child(child, 0)
-
-    @pl.loop(1, devices)
-    def _(step):
-        d = (me + step) % devices
-        replied(d).wait_recv()
-
-    @pl.loop(0, child_dev)
-    def _(child):
-        value = o_in[plan[src_at + child]].astype(jnp.float32)
-        put_attended(res_rows + child, jnp.where(plan[which_at + child] == 1, value[20:40], value[0:20]))
-
-    @pl.loop(0, per_group)
-    def _(c):
-        main[-1].arrive(c)
-
-    @pl.loop(0, child_dev)
-    def _(child):
-        update_child(child, GROUPS - 1)
+                    serve([(tick - 2) * batch + i])
+
+            @pl.when(tick == ready)
+            def _():
+                side.arrive(0)
+                convolve()
+
+                @pl.loop(0, res_rows)
+                def _(row):
+                    update_resident([row])
+
+            if groups > 1:
+
+                @pl.when(tick == landed_at)
+                def _():
+                    @pl.loop(0, per_group)
+                    def _(c):
+                        main[0].arrive(c)
+
+                @pl.when(tick >= landed_at)
+                def _():
+                    @pl.loop(0, share)
+                    def _(i):
+                        child = (tick - landed_at) * share + i
+
+                        @pl.when(child < child_dev)
+                        def _():
+                            update_child([child], 0)
+
+        @pl.loop(0, per_group)
+        def _(c):
+            main[-1].arrive(c)
+
+    def run_routes():
+        span = X_START + X_SLOTS + LAG
+        children = span + 1 + -(-res_rows // 2)
+        serve_from = 8
+        wait = -(-child_dev // 4)
+        ticks = (groups - 1) * STRIDE + span
+
+        @pl.loop(0, ticks)
+        def _(tick):
+            for i in range(groups):
+                main[i].z_step(tick - i * STRIDE)
+            side.z_step(tick)
+            for i in range(groups):
+                main[i].x_step(tick - i * STRIDE)
+            side.x_step(tick)
+            pl.when(tick == 0)(prepare)
+            spread_over(tick, 1, 1, devices, ask)
+            spread_over(tick, 9, 4, res_rows, resident)
+            spread_over(tick, serve_from, 1, devices, serve)
+            pl.when(tick == span)(convolve)
+            spread_over(tick, span + 1, 2, res_rows, update_resident)
+            for i in range(groups - 1):
+                start = max(children + i * wait, i * STRIDE + span)
+                spread_over(tick, start, 4, child_dev, functools.partial(update_child, i=i))
+            pl.when(tick == ticks - span + SLOTS + REPLY)(reply_all)
+
+    if routed:
+        run_routes()
+    else:
+        run_ring()
+
+    @pl.loop(0, child_dev // 4)
+    def _(part):
+        update_child([4 * part + j for j in range(4)], groups - 1)
 
     gated = []
     gates = g_v[...].astype(jnp.float32)
+    reads = read[...]
     lane = lax.broadcasted_iota(jnp.int32, (rows, 128), 1)
     total = jnp.zeros((rows, 128), jnp.float32)
     for t in range(STEPS):
-        value = (carried[t] * read[t] + rest[t]) * silu(gates[:, t, :])
+        value = (carried[t] * reads[:, t, :] + rest[t]) * silu(gates[:, t, :])
         gated.append(value)
         total = jnp.where(lane == t, jnp.sum(value * value, 1, keepdims=True), total)
     sums[...] = total
@@ -591,7 +775,8 @@
         def _(step):
             share_sums((tensor + step) % peers, tensor).start()
 
-    for stream, count in [(side, 1)] + [(m, per_group) for m in main]:
+    gather_replies()
+    for stream, count in [(side, 1)] + [(m, 1 if routed else per_group) for m in main]:
 
         @pl.loop(0, count)
         def _(c):
@@ -600,7 +785,7 @@
     @pl.loop(1, devices)
     def _(step):
         d = (me + step) % devices
-        ask(d).wait_send()
+        asking(d).wait_send()
         reply(d).wait_send()
 
     if peers > 1:
@@ -625,7 +810,7 @@
 
     @pl.loop(0, rows)
     def _(row):
-        for i in range(GROUPS):
+        for i in range(groups):
             new_copy(row, i).wait()
 
     if peers > 1:
@@ -635,7 +820,7 @@
             share_sums((tensor + step) % peers, tensor).wait_send()
 
 
-def run_round(plan, scalars, arrays, ring, peers):
+def run_round(plan, routes, scalars, arrays, ring, peers, routed):
     slots = Slots(ring)
     half = ring // 2
     devices = COLUMNS * ring
@@ -644,7 +829,8 @@
     rows, res_rows = queries.shape[0], res.shape[0]
     child_dev = rows - res_rows
     features = heads * SSM_HEAD
-    per_group = heads // GROUPS
+    groups = len(ROUTE_HEADS) if routed else RING_GROUPS
+    per_group = heads // groups
     bf16, f32 = jnp.bfloat16, jnp.float32
     dma = pltpu.SemaphoreType.DMA
 
@@ -677,7 +863,7 @@
         pltpu.VMEM((16, rows, features), f32),
         pltpu.VMEM((STEPS, rows, features), f32),
         pltpu.VMEM((STEPS, rows, features), f32),
-        pltpu.VMEM((STEPS, rows, features), f32),
+        pltpu.VMEM((rows, 8, features), f32),
     ]
     scratch += [
         pltpu.VMEM((devices, PAIR, HEAD), bf16),
@@ -690,29 +876,224 @@
         pltpu.VMEM((peers, rows, 128), f32),
         dma((peers,)),
         dma((peers,)),
-        dma((rows, GROUPS)),
+        dma((rows, groups)),
     ]
-    for _ in range(GROUPS):
-        scratch += stream(per_group, SSM_HEAD)
-    scratch += stream(1, 16)
+    def route(count, height):
+        packets = 2 * (SLOTS + X_SLOTS)
+        return [
+            pltpu.VMEM((packets, count, height, STATE), bf16),
+            pltpu.VMEM((packets, count, height, STATE), bf16),
+            dma((2, SLOTS)), dma((2, SLOTS)), dma((2, X_SLOTS)), dma((2, X_SLOTS)),
+        ]
+
+    for _ in range(groups):
+        scratch += route(ROUTE_HEADS[_], SSM_HEAD) if routed else stream(per_group, SSM_HEAD)
+    scratch += (route if routed else stream)(1, 16)
     smem = pl.BlockSpec(memory_space=pltpu.SMEM)
     vmem = pl.BlockSpec(memory_space=pltpu.VMEM)
     anywhere = pl.BlockSpec(memory_space=pl.ANY)
     return pl.pallas_call(
-        functools.partial(round_kernel, slots, heads, res_rows, child_dev, peers),
+        functools.partial(round_kernel, slots, heads, res_rows, child_dev, peers, routed),
         out_shape=[
             jax.ShapeDtypeStruct(queries.shape, bf16),
             jax.ShapeDtypeStruct((STEPS, rows, features), bf16),
             jax.ShapeDtypeStruct((rows,) + ssm.shape[1:], bf16),
         ],
-        in_specs=[smem] * (1 + len(scalars)) + [anywhere] * len(arrays),
+        in_specs=[smem] * (2 + len(scalars)) + [anywhere] * len(arrays),
         out_specs=[vmem, vmem, anywhere],
         scratch_shapes=scratch,
         compiler_params=pltpu.CompilerParams(
-            collective_id=0, has_side_effects=True, vmem_limit_bytes=60 * 1024 * 1024
+            collective_id=1 if routed else 0, has_side_effects=True, vmem_limit_bytes=60 * 1024 * 1024
         ),
-        name="round",
-    )(plan, *scalars, *arrays)
+        name="routed_round" if routed else "ring_round",
+    )(plan, routes, *scalars, *arrays)
+
+
+def plan_routes(parents, ops, S, L, X0, NX):
+    where, rollx, rollz, srl, orall, const, lanes = ops
+    x, z = (lanes >> 3) & 3, lanes & 7
+    kids = []
+    zero = const(0)
+    need = [zero, zero, zero, zero]
+    for p in parents:
+        src, n = p >> 2, p & 3
+        dx, dz = ((src >> 3) - x) & 3, ((src & 7) - z) & 7
+        bit = const(1) << (n * 8 + dz)
+        kids.append((dx, dz, n, bit))
+        for k in range(4):
+            need[k] = need[k] | where(dx == k, bit, zero)
+    need = [orall(v) for v in need]
+    me_, across, right, left = need[0], rollx(need[2], 2), rollx(need[3], -1), rollx(need[1], 1)
+    row = me_ | across | right | left
+    D4, D5, D3 = 0x10101010, 0x20202020, 0x08080808
+    UPB, DNB = 0xE0E0E0E0 - (1 << 32), 0x0E0E0E0E
+    D0 = 0x01010101
+    ev = 0x00100010
+    opp = row & D4
+    up_near, dn_near = zero, zero
+    go_up, go_dn = zero, zero
+    from_below, from_above = row, row
+    for k in (1, 2, 3):
+        from_below, from_above = rollz(from_below, 1), rollz(from_above, -1)
+        up_near = up_near | (srl(from_below, k) & opp)
+        dn_near = dn_near | ((from_above << k) & opp)
+        go_up = go_up | (up_near & ~dn_near)
+        go_dn = go_dn | (dn_near & ~up_near)
+    go_up = go_up | (opp & ~go_dn & ev)
+    need_up = (row & UPB) | go_up
+    need_dn = (row & DNB) | (opp & ~go_up)
+
+    def sender_up(m):
+        return srl(m & (0x80808080 - (1 << 32)), 7) & D0 | ((m & 0x70707070) << 1)
+
+    def receiver_up(m):
+        return ((m & D0) << 7) | srl(m & UPB, 1)
+
+    def sender_dn(m):
+        return srl(m & (DNB | D4), 1)
+
+    def receiver_dn(m):
+        return m << 1
+
+    todo_all = zero
+    C, U = {}, {}
+    for name, wanted, step, send, recv, keep in (
+        ("up", need_up, 1, sender_up, receiver_up, UPB),
+        ("dn", need_dn, -1, sender_dn, receiver_dn, DNB),
+    ):
+        A = [send(rollz(wanted, -step))]
+        for _ in range(3):
+            A.append(send(rollz(A[-1] & keep, -step)))
+        act = A[0] | A[1] | A[2] | A[3]
+        ready = act & D0
+        todo = act
+        come = {}
+        C[name], U[name] = [], []
+        for s in range(S):
+            if s in come:
+                ready = ready | (come[s] & act)
+            best = ready & A[3]
+            for k in (2, 1, 0):
+                best = where(best != 0, best, ready & A[k])
+            pick = best & -best
+            ready = ready & ~pick
+            todo = todo & ~pick
+            got = rollz(recv(pick), step)
+            C[name].append(pick)
+            U[name].append(got)
+            come[s + L] = got
+        todo_all = todo_all | todo
+    EVEN = 0x55555555
+    first_p = (across & right) | (across & ~left & EVEN)
+    first_m = across & ~first_p
+    direct_p, direct_m = right & ~first_p, left & ~first_m
+    X = {}
+    for name, step, direct, first in (("p", 1, direct_p, first_p), ("m", -1, direct_m, first_m)):
+        arrived = {}
+        second = rollx(first, step)
+        todo1, todo2, todod = first, second, direct
+        have = D0 | zero
+        got2 = zero
+        come = {}
+        X[name] = []
+        for t in range(X0 + NX):
+            s = t - L
+            if 0 <= s < S:
+                have = have | U["up"][s] | U["dn"][s]
+            if t in come:
+                got2 = got2 | come[t]
+            if t < X0:
+                continue
+            r1, r2, rd = todo1 & have, todo2 & got2, todod & have
+            p1 = r1 & -r1
+            none = r1 == 0
+            p2 = where(none, r2 & -r2, zero)
+            none = none & (r2 == 0)
+            pd = where(none, rd & -rd, zero)
+            todo1, todo2, todod = todo1 & ~p1, todo2 & ~p2, todod & ~pd
+            come[t + L] = rollx(p1, step)
+            X[name].append((p1 | pd, p2, rollx(p1 | pd, step), rollx(p2, step)))
+        todo_all = todo_all | todo1 | todo2 | todod
+    def node(m):
+        return where((m & 0x0000FF00) != 0, const(1), zero) + where((m & 0x00FF0000) != 0, const(2), zero) + where(srl(m, 24) != 0, const(3), zero)
+
+    tables = []
+    for base, name in ((0, "up"), (S, "dn")):
+        for s in range(S):
+            code = node(C[name][s])
+            for r in range(0, s - L + 1):
+                same = (C[name][s] & U[name][r]) != 0
+                code = where(same, const(4 + base + r), code)
+            tables.append(code)
+    for base, name in ((2 * S, "p"), (2 * S + NX, "m")):
+        for i in range(NX):
+            here, passing = X[name][i][0], X[name][i][1]
+            code = node(here)
+            for r in range(0, min(X0 + i - L + 1, S)):
+                code = where((here & U["up"][r]) != 0, const(4 + r), code)
+                code = where((here & U["dn"][r]) != 0, const(4 + S + r), code)
+            for r in range(0, i - L + 1):
+                code = where((passing & X[name][r][2]) != 0, const(4 + base + r), code)
+            tables.append(code)
+    places = []
+    for dx, dz, n, bit in kids:
+        code = where((dx == 0) & (dz == 0), n, const(-1))
+        for r in range(S):
+            code = where((dx == 0) & ((bit & U["up"][r]) != 0), const(4 + r), code)
+            code = where((dx == 0) & ((bit & U["dn"][r]) != 0), const(4 + S + r), code)
+        for r in range(NX):
+            code = where(((dx == 3) & ((bit & X["p"][r][2]) != 0)) | ((dx == 2) & ((bit & X["p"][r][3]) != 0)), const(4 + 2 * S + r), code)
+            code = where(((dx == 1) & ((bit & X["m"][r][2]) != 0)) | ((dx == 2) & ((bit & X["m"][r][3]) != 0)), const(4 + 2 * S + NX + r), code)
+        places.append(code)
+    return tables, places, todo_all
+
+
+def plan_kernel(parents, routes):
+    shape = (8, 128)
+    lane = lax.broadcasted_iota(jnp.int32, shape, 1)
+    row = (lane & 7)
+
+    def rollx(value, by):
+        return pltpu.roll(value, (8 * by) % 128, 1)
+
+    def rollz(value, by):
+        if by == 1:
+            return jnp.where(row >= 1, pltpu.roll(value, 1, 1), pltpu.roll(value, 121, 1))
+        return jnp.where(row < 7, pltpu.roll(value, 127, 1), pltpu.roll(value, 7, 1))
+
+    def or_all(value):
+        for by in (4, 2, 1):
+            value = value | pltpu.roll(value, by, 0)
+        return value
+
+    def constant(value):
+        return jnp.full(shape, value, jnp.int32)
+
+    ops = (jnp.where, rollx, rollz, lax.shift_right_logical, or_all, constant, lane)
+    kids = [parents[i : i + 8] for i in range(0, parents.shape[0], 8)]
+    tables, places, left_over = plan_routes(kids, ops, SLOTS, LAG, X_START, X_SLOTS)
+    bad = left_over != 0
+    for i, table in enumerate(tables):
+        routes[i : i + 1] = table[0:1]
+    for i, place in enumerate(places):
+        start = PLACE_ROW + 8 * i
+        routes[start : start + 8] = jnp.maximum(place, 0)
+        bad = bad | (place < 0)
+    bad = jnp.max(jnp.where(bad, 1.0, 0.0), axis=1, keepdims=True)
+    bad = jnp.max(bad, axis=0, keepdims=True)
+    last = PLACE_ROW + parents.shape[0]
+    routes[last : last + 1] = jnp.where(jnp.broadcast_to(bad, (1, 128)) > 0.0, 1, 0)
+
+
+def find_routes(parents, devices):
+    children = parents.shape[0] // devices
+    lines = jnp.tile(parents.reshape(devices, children).T, (1, 128 // devices))
+    routes = pl.pallas_call(
+        plan_kernel,
+        out_shape=jax.ShapeDtypeStruct((PLACE_ROW + children + 2, 128), jnp.int32),
+        name="find_routes",
+    )(lines)
+    return routes, routes[PLACE_ROW + children, 0] == 0
 
 
 def per_device(
@@ -747,7 +1128,13 @@
         jnp.transpose(dt_in, (1, 2, 0)), *turned, conv_x_weight, conv_bc_weight, norm_gain[None, :],
     ]
     scalars = [len_nodes, len_resident, alive_flags, a_log, dt_bias, skip_gain]
-    attn, ssm_out, new_ssm = run_round(plan, scalars, arrays, ring, lax.axis_size("tensor"))
+    peers = lax.axis_size("tensor")
+    routes, fits = find_routes(parents, devices)
+
+    def go(routed):
+        return lambda p, r, s, a: tuple(run_round(p, r, s, a, ring, peers, routed))
+
+    attn, ssm_out, new_ssm = lax.cond(fits, go(True), go(False), plan, routes, scalars, arrays)
     return attn, jnp.transpose(ssm_out, (1, 0, 2)), new_ssm
 
 

time: 159 us -> 142 us (0.89)
  Pallas kernels: 145 us -> 128 us
    pallas_call x1, Pallas kernels: 145 us -> 125 us  [run_round(): pl.pallas_call(functools.partial(round_kernel, slots, heads, res_rows, ch...]
    unnamed x3 -> x2, local copies, waits for them, and re-layouts: 9.79 us -> 7.26 us
    pallas_call x0 -> x1, Pallas kernels: none -> 2.06 us  [find_routes(): pl.pallas_call(plan_kernel, out_shape=jax.ShapeDtypeStruct((PLACE_ROW + c...]
where the time goes in v3:
time: 142 us; the launch traced here: 141 us
  Pallas kernels  128 us (90%)
  local copies, waits for them, and re-layouts  10.2 us (7%)
  other arithmetic  2.1 us (1%)
    pallas_call x1, Pallas kernels, run_round(): pl.pallas_call(functools.partial(round_kernel, slots, heads, res_rows, ch...  125 us
    unnamed x2, local copies, waits for them, and re-layouts  7.26 us

profile of v3, /device:TPU:1, one launch (start us, length us, event | category | flops | bytes accessed | tf_op | source)
XLA Modules:
  0.0 141.3 jit_solution(9350867519765631144)
XLA Ops:
  0.7 0.8 fusion.3
  1.4 0.8 select_reduce_fusion.4
  2.3 0.1 select_reduce_fusion.3
  2.4 0.1 select_reduce_fusion.1
  2.5 0.8 reshape.74
  3.3 0.1 copy.33
  3.4 0.7 tile.10.parents
  4.0 2.1 %find_routes.1 = s32[64,128]{1,0:T(8,128)S(1)} custom-call(s32[16,128]{1,0:T(8,128)} %tile.10.parents), custom_call_target="tpu_custom_call" | custom-call | tf_op jit(solution)/shard_map/find_routes/pallas_call | solution.py:1091
  6.1 0.5 slice.4
  7.3 0.2 select_reduce_fusion
  7.5 0.1 reshape.75
  7.6 0.1 concatenate.3
  7.7 125.6 %conditional.1 = ((bf16[24,4,640]{2,1,0:T(4,128)(2,1)S(1)}, bf16[4,24,512]{2,1,0:T(8,128)(2,1)S(1)}, bf16[24,8,64,256]{3,2,1,0:T(8,128)(2,1)})) conditional(s32[]{:T(128)} %bitcast.1, (s32[1136]{0:T(1024)S(1)}, s32[64,128]{1,0:T(8,128)S(1)}, s32[128]{0:T(128)}, s32[8]{0:T(128)}, s32[24]{0:T(128)}, /*index=5*/f32[8]{0:T(128)}, f32[8]{0:T(128)}, ...), branch_computations={%region_5.6_spmd, %region_6.7_spmd} | conditional | bytes 8 | solution.py:1137
  7.8 125.5 %routed_round.1 = (bf16[24,4,640]{2,1,0:T(4,128)(2,1)S(1)}, bf16[4,24,512]{2,1,0:T(8,128)(2,1)S(1)}, bf16[24,8,64,256]{3,2,1,0:T(8,128)(2,1)}) custom-call(s32[1136]{0:T(1024)S(1)} %get-tuple-element.125.plan, s32[64,128]{1,0:T(8,128)S(1)} %get-tuple-element.126.routes, s32[128]{0:T(128)} %get-tuple-element.127.len_nodes, s32[8]{0:T(128)} %get-tuple-element.128.len_res, ...), custom_call_target="tpu_custom_call" | custom-call | tf_op jit(solution)/shard_map/cond/branch_1_fun/routed_round/pallas_call | solution.py:895
  133.3 0.7 copy.36
  134.0 0.6 copy.45
  134.7 6.6 %copy.46 = bf16[24,8,64,256]{3,2,1,0:T(8,128)(2,1)} copy(bf16[24,8,64,256]{3,2,1,0:T(8,128)(2,1)} %get-tuple-element.176) | data formatting | bytes 12582912
  (2 shorter events, 0.0 us)

commit v4 on v3

--- a/solution.py
+++ b/solution.py
@@ -62,6 +62,7 @@
 PAIR = 64
 BACK = 48
 BLOCK = 32
+PAIR_DEVICES = 32
 RING_GROUPS = 2
 ROUTE_HEADS = (2, 2, 2, 2)
 
@@ -69,6 +70,7 @@
 REPLY = 0
 STRIDE = 12
 PLACE_ROW = 2 * (SLOTS + X_SLOTS)
+SRC_ROW, WHICH_ROW, FITS_ROW, PAIR_ROW = PLACE_ROW + 16, PLACE_ROW + 32, PLACE_ROW + 48, PLACE_ROW + 56
 
 
 def dot(a, b, dims):
@@ -456,7 +458,11 @@
         messages = []
         for step in steps:
             d = (me + step) % devices
-            messages.append(pack(res_rows + plan[first_at + d], res_rows + plan[second_at + d]))
+            if routed:
+                first, second = routes[PAIR_ROW + devices + d, me], routes[PAIR_ROW + 2 * devices + d, me]
+            else:
+                first, second = plan[first_at + d], plan[second_at + d]
+            messages.append(pack(res_rows + first, res_rows + second))
         for step, message in zip(steps, messages):
             d = (me + step) % devices
 
@@ -479,7 +485,7 @@
 
         results = []
         for d in served:
-            node = plan[d * devices + me]
+            node = routes[PAIR_ROW + me, d] if routed else plan[d * devices + me]
             length = len_nodes[me * NODE_DEV + node]
             result = attend(q_in[d], kv_nodes[node, 0], kv_nodes[node, 1], length)
             results.append(result[:BACK].astype(jnp.bfloat16))
@@ -641,8 +647,12 @@
 
         @pl.loop(0, child_dev)
         def _(child):
-            value = o_in[plan[src_at + child]].astype(jnp.float32)
-            put_attended(res_rows + child, jnp.where(plan[which_at + child] == 1, value[20:40], value[0:20]))
+            if routed:
+                source, which = routes[SRC_ROW + child, me], routes[WHICH_ROW + child, me]
+            else:
+                source, which = plan[src_at + child], plan[which_at + child]
+            value = o_in[source].astype(jnp.float32)
+            put_attended(res_rows + child, jnp.where(which == 1, value[20:40], value[0:20]))
 
     def run_ring():
         batch = 4
@@ -1081,8 +1091,34 @@
         bad = bad | (place < 0)
     bad = jnp.max(jnp.where(bad, 1.0, 0.0), axis=1, keepdims=True)
     bad = jnp.max(bad, axis=0, keepdims=True)
-    last = PLACE_ROW + parents.shape[0]
-    routes[last : last + 1] = jnp.where(jnp.broadcast_to(bad, (1, 128)) > 0.0, 1, 0)
+    routes[FITS_ROW : FITS_ROW + 8] = jnp.where(jnp.broadcast_to(bad, shape) > 0.0, 1, 0)
+
+    def over(value, pick):
+        for by in (4, 2, 1):
+            value = pick(value, pltpu.roll(value, by, 0))
+        return value
+
+    line = lax.broadcasted_iota(jnp.int32, shape, 0)
+    index = [line + 8 * i for i in range(len(kids))]
+    which = [constant(0) for _ in kids]
+    count = PAIR_DEVICES
+    for source in range(count):
+        here = [(kid >> 2) == source for kid in kids]
+
+        def gather(values, other, pick):
+            parts = [jnp.where(at, value, other) for at, value in zip(here, values)]
+            return over(functools.reduce(pick, parts), pick)
+
+        first = gather(index, 8 * len(kids) - 1, jnp.minimum)
+        for i, value in enumerate((
+            gather([kid & 3 for kid in kids], 0, jnp.maximum), first, gather(index, 0, jnp.maximum),
+        )):
+            at_row = PAIR_ROW + i * count + source
+            routes[at_row : at_row + 1] = value[0:1]
+        which = [jnp.where(at & (i > first), 1, w) for at, i, w in zip(here, index, which)]
+    for i, kid in enumerate(kids):
+        routes[SRC_ROW + 8 * i : SRC_ROW + 8 * i + 8] = kid >> 2
+        routes[WHICH_ROW + 8 * i : WHICH_ROW + 8 * i + 8] = which[i]
 
 
 def find_routes(parents, devices):
@@ -1090,10 +1126,10 @@
     lines = jnp.tile(parents.reshape(devices, children).T, (1, 128 // devices))
     routes = pl.pallas_call(
         plan_kernel,
-        out_shape=jax.ShapeDtypeStruct((PLACE_ROW + children + 2, 128), jnp.int32),
+        out_shape=jax.ShapeDtypeStruct((PAIR_ROW + 3 * devices, 128), jnp.int32),
         name="find_routes",
     )(lines)
-    return routes, routes[PLACE_ROW + children, 0] == 0
+    return routes, routes[FITS_ROW, 0] == 0
 
 
 def per_device(
@@ -1106,22 +1142,24 @@
     ring = devices // COLUMNS
     child_dev = parents.shape[0] // devices
 
-    grouped = parents.reshape(devices, child_dev)
-    match = (grouped // NODE_DEV)[:, None, :] == jnp.arange(devices)[None, :, None]
-    tab = jnp.max(jnp.where(match, (grouped % NODE_DEV)[:, None, :], 0), axis=2).reshape(-1)
-    own = lax.dynamic_slice_in_dim(parents, me * child_dev, child_dev)
-    child_src = own // NODE_DEV
-    mine = child_src[None, :] == jnp.arange(devices)[:, None]
-    number = jnp.arange(child_dev)[None, :]
-    first = jnp.min(jnp.where(mine, number, child_dev - 1), axis=1)
-    second = jnp.max(jnp.where(mine, number, 0), axis=1)
-    child_which = jnp.sum(jnp.where(mine & (number > first[:, None]), 1, 0), axis=0)
-    relative = (
-        (child_src // ring - me // ring) % COLUMNS * ring + (child_src % ring - me % ring) % ring
-    )
-    spot = jnp.arange(devices)[None, :] == relative[:, None]
-    place = jnp.sum(jnp.where(spot, jnp.asarray(Slots(ring).table())[None, :], 0), axis=1)
-    plan = jnp.concatenate([tab, first, second, child_src, child_which, place]).astype(jnp.int32)
+    def ring_plan(parents):
+        grouped = parents.reshape(devices, child_dev)
+        match = (grouped // NODE_DEV)[:, None, :] == jnp.arange(devices)[None, :, None]
+        tab = jnp.max(jnp.where(match, (grouped % NODE_DEV)[:, None, :], 0), axis=2).reshape(-1)
+        own = lax.dynamic_slice_in_dim(parents, me * child_dev, child_dev)
+        child_src = own // NODE_DEV
+        mine = child_src[None, :] == jnp.arange(devices)[:, None]
+        number = jnp.arange(child_dev)[None, :]
+        first = jnp.min(jnp.where(mine, number, child_dev - 1), axis=1)
+        second = jnp.max(jnp.where(mine, number, 0), axis=1)
+        child_which = jnp.sum(jnp.where(mine & (number > first[:, None]), 1, 0), axis=0)
+        relative = (
+            (child_src // ring - me // ring) % COLUMNS * ring + (child_src % ring - me % ring) % ring
+        )
+        spot = jnp.arange(devices)[None, :] == relative[:, None]
+        place = jnp.sum(jnp.where(spot, jnp.asarray(Slots(ring).table())[None, :], 0), axis=1)
+        return jnp.concatenate([tab, first, second, child_src, child_which, place]).astype(jnp.int32)
+
     turned = [jnp.transpose(a, (1, 0, 2)) for a in (conv_resident, convbc_resident, conv_nodes, convbc_nodes)]
     arrays = [
         ssm_nodes, ssm_resident, kv_nodes, kv_resident, queries, new_kv, x_in, gate_in, bc_in,
@@ -1131,10 +1169,13 @@
     peers = lax.axis_size("tensor")
     routes, fits = find_routes(parents, devices)
 
-    def go(routed):
-        return lambda p, r, s, a: tuple(run_round(p, r, s, a, ring, peers, routed))
-
-    attn, ssm_out, new_ssm = lax.cond(fits, go(True), go(False), plan, routes, scalars, arrays)
+    def by_routes(p, r, s, a):
+        return tuple(run_round(s[0], r, s, a, ring, peers, True))
+
+    def by_ring(p, r, s, a):
+        return tuple(run_round(ring_plan(p), r, s, a, ring, peers, False))
+
+    attn, ssm_out, new_ssm = lax.cond(fits, by_routes, by_ring, parents, routes, scalars, arrays)
     return attn, jnp.transpose(ssm_out, (1, 0, 2)), new_ssm
 
 

time: 142 us -> 141 us (level)
  other arithmetic: 2.1 us -> 0 us
where the time goes in v4:
time: 141 us; the launch traced here: 140 us
  Pallas kernels  129 us (91%)
  local copies, waits for them, and re-layouts  10 us (7%)
    pallas_call x1, Pallas kernels, run_round(): pl.pallas_call(functools.partial(round_kernel, slots, heads, res_rows, ch...  127 us
    unnamed x2, local copies, waits for them, and re-layouts  7.26 us

profile of v4, /device:TPU:1, one launch (start us, length us, event | category | flops | bytes accessed | tf_op | source)
XLA Modules:
  0.0 140.4 jit_solution(6901463999084978624)
XLA Ops:
  0.6 0.8 reshape.76
  1.4 0.1 copy.33
  1.5 0.7 tile.10.parents
  2.2 2.3 %find_routes.1 = s32[198,128]{1,0:T(8,128)S(1)} custom-call(s32[16,128]{1,0:T(8,128)} %tile.10.parents), custom_call_target="tpu_custom_call" | custom-call | tf_op jit(solution)/shard_map/find_routes/pallas_call | solution.py:1127
  4.4 0.5 slice.4
  5.6 126.8 %conditional.1 = ((bf16[24,4,640]{2,1,0:T(4,128)(2,1)S(1)}, bf16[4,24,512]{2,1,0:T(8,128)(2,1)S(1)}, bf16[24,8,64,256]{3,2,1,0:T(8,128)(2,1)})) conditional(s32[]{:T(128)} %bitcast.1, (s32[512]{0:T(512)}, s32[]{:T(128)}, s32[198,128]{1,0:T(8,128)S(1)}, s32[128]{0:T(128)}, s32[8]{0:T(128)}, /*index=5*/s32[24]{0:T(128)}, f32[8]{0:T(128)}, ...), branch_computations={%region_0.6_spmd.clone, %region_6.7_spmd} | conditional | flops 65399 | bytes 36989 | solution.py:1178
  5.8 126.6 %routed_round.1 = (bf16[24,4,640]{2,1,0:T(4,128)(2,1)S(1)}, bf16[4,24,512]{2,1,0:T(8,128)(2,1)S(1)}, bf16[24,8,64,256]{3,2,1,0:T(8,128)(2,1)}) custom-call(s32[128]{0:T(128)} %get-tuple-element.129.plan.len_nodes, s32[198,128]{1,0:T(8,128)S(1)} %get-tuple-element.130.routes, s32[128]{0:T(128)} %get-tuple-element.129.plan.len_nodes, ...), custom_call_target="tpu_custom_call" | custom-call | tf_op jit(solution)/shard_map/cond/branch_1_fun/routed_round/pallas_call | solution.py:905
  132.4 0.7 copy.36
  133.1 0.6 copy.45
  133.7 6.6 %copy.46 = bf16[24,8,64,256]{3,2,1,0:T(8,128)(2,1)} copy(bf16[24,8,64,256]{3,2,1,0:T(8,128)(2,1)} %get-tuple-element.233) | data formatting | bytes 12582912
  (1 shorter events, 0.0 us)
